TPU v7x, 256 devices: a whole 4x4x8 slice. The times are simulated.
256 devices in a mesh: dom: 256 (over z, x, y, core).
Axes of the slice: x: 4, y: 4, z: 8, core: 2. Of those that a mesh axis runs over, the one named last changes fastest.
Arguments:
- embeddings: float32 [65536, 400], P('dom')
- entity_state: float32 [65536], P('dom'), may hold values from 0.0001 to 0.01
- relations: float32 [1300, 400], replicated, may hold values from 0.1 to 1.9
- relation_state: float32 [1300], replicated, may hold values from 0.01 to 1
- round_masks: int32 [2], replicated, may hold values from 1 to 255
- edge_src: int32 [2, 32768], P(None, 'dom'), may hold values from 0 to 255
- edge_rel: int32 [2, 32768], P(None, 'dom'), may hold values from 0 to 1299
- edge_dst: int32 [2, 32768], P(None, 'dom'), may hold values from 0 to 255
- edge_count: int32 [2, 256], P(None, 'dom'), may hold values from 64 to 128, as said below
- neg_rows: int32 [2, 256, 1000], P(None, 'dom'), may hold values from 0 to 255
Outputs:
- new_embeddings: float32 [65536, 400], P('dom')
- new_entity_state: float32 [65536], P('dom')
- new_relations: float32 [1300, 400], replicated
- new_relation_state: float32 [1300], replicated
Inputs may be any that keep to these rules, and one draw needn't show every extreme that they name: In round r, device p (partition p) trains the bucket of its own partition with partition p XOR round_masks[r]. A bucket's live edges are its first edge_count slots; in every round some device has exactly 128. `edge_src`: rows of the device's own partition; slots past the count are padding. `edge_dst`: rows of the partner partition of that round. `neg_rows`: row p + c lists the negatives of block c of device p, as rows of the partner partition.
All inputs are finite; a program needn't handle non-finite values.
Results may differ from a plain program's by a relative error of at most 0.0033.
The roundings to bfloat16 on the way count: a program that leaves them out, or rounds other values in their place, can miss the bound.
Values may be sent and summed in bfloat16 or wider, within the bound.
A program may use at most 64 MiB of HBM per device.

v0:
```python
import jax
import jax.numpy as jnp
from jax import lax
from jax.sharding import PartitionSpec as P

ROUNDS = 2


learning_rate = 0.1


def from_partner(value, axis, distance):
    mask = 2**distance
    pairs = [(source, source ^ mask) for source in range(lax.axis_size(axis))]
    return lax.ppermute(value, axis, pairs)


def bit_is_set(round_mask, hop_index):
    return jnp.bitwise_and(jnp.right_shift(round_mask, hop_index), 1) == 1


def rows_across(payload, round_mask):
    for hop_index in range(lax.axis_size("dom").bit_length() - 1):
        moved = from_partner(payload, "dom", hop_index)
        payload = jnp.where(bit_is_set(round_mask, hop_index), moved, payload)
    return payload


def grads_across(payload, round_mask):
    for hop_index in range(lax.axis_size("dom").bit_length() - 1):
        moved = from_partner(payload, "dom", hop_index)
        payload = jnp.where(bit_is_set(round_mask, hop_index), moved, payload)
    return payload


def bucket_grads(vectors, dst_ids, live_edges, neg_ids, table):
    groups, negatives = neg_ids.shape
    edge_total, features = vectors.shape
    per_group = edge_total // groups
    target = table[dst_ids]
    positive = jnp.einsum("ed,ed->e", vectors, target, preferred_element_type=jnp.float32)
    pos_coef = -live_edges * jax.nn.sigmoid(-positive)
    blocks = vectors.reshape(groups, per_group, features)
    neg_table = table[neg_ids]
    scores = jnp.einsum("ced,cnd->cen", blocks, neg_table, preferred_element_type=jnp.float32)
    neg_coef = (
        live_edges.reshape(groups, per_group, 1) * jax.nn.sigmoid(scores) / negatives
    ).astype(jnp.bfloat16)
    neg_pull = jnp.einsum(
        "cen,cnd->ced", neg_coef, neg_table, preferred_element_type=jnp.float32
    ).reshape(edge_total, features)
    vec_grads = (pos_coef[:, None] * target.astype(jnp.float32) + neg_pull).astype(jnp.bfloat16)
    row_terms = jnp.einsum(
        "cen,ced->cnd", neg_coef, blocks, preferred_element_type=jnp.float32
    ).reshape(groups * negatives, features)
    dest_grads = jnp.zeros((table.shape[0], features), jnp.float32)
    dest_grads = dest_grads.at[dst_ids].add(pos_coef[:, None] * vectors.astype(jnp.float32))
    dest_grads = dest_grads.at[neg_ids.reshape(-1)].add(row_terms)
    return (vec_grads, dest_grads.astype(jnp.bfloat16))


def shards(
    embeddings,
    entity_state,
    relations,
    relation_state,
    round_masks,
    edge_src,
    edge_rel,
    edge_dst,
    edge_count,
    neg_rows,
):
    entity_rows = embeddings
    row_state = entity_state
    rel_total = jnp.zeros(relations.shape, jnp.float32)
    edge_total = edge_src.shape[1]
    slot_index = jnp.arange(edge_total, dtype=jnp.int32)
    for round_index in range(ROUNDS):
        round_mask = round_masks[round_index]
        src_ids = edge_src[round_index]
        rel_ids = edge_rel[round_index]
        dst_ids = edge_dst[round_index]
        neg_ids = neg_rows[round_index]
        live_edges = (slot_index < edge_count[round_index, 0]).astype(jnp.float32)
        rows_bf = entity_rows.astype(jnp.bfloat16)
        src_rows = entity_rows[src_ids]
        rel_rows = relations[rel_ids]
        vectors = (src_rows * rel_rows).astype(jnp.bfloat16)
        partner_bf = rows_across(rows_bf, round_mask)
        vec_grads, sent_grads = bucket_grads(vectors, dst_ids, live_edges, neg_ids, partner_bf)
        dest_mine = grads_across(sent_grads, round_mask)
        grad_wide = vec_grads.astype(jnp.float32)
        src_grads = jnp.zeros(entity_rows.shape, jnp.float32).at[src_ids].add(grad_wide * rel_rows)
        rel_round = jnp.zeros(relations.shape, jnp.float32).at[rel_ids].add(grad_wide * src_rows)
        rel_total = rel_total + rel_round
        row_grads = src_grads + dest_mine.astype(jnp.float32)
        row_state = row_state + jnp.mean(row_grads * row_grads, axis=1)
        entity_rows = entity_rows - learning_rate * row_grads / jnp.sqrt(row_state)[:, None]
    rel_total = lax.psum(rel_total, "dom")
    new_state = relation_state + jnp.mean(rel_total * rel_total, axis=1)
    new_relations = relations - learning_rate * rel_total / jnp.sqrt(new_state)[:, None]
    return (entity_rows, row_state, new_relations, new_state)


def solution(mesh):
    placed = (
        P("dom", None),
        P("dom"),
        P(),
        P(),
        P(),
        P(None, "dom"),
        P(None, "dom"),
        P(None, "dom"),
        P(None, "dom"),
        P(None, "dom", None),
    )
    return jax.shard_map(
        shards,
        mesh=mesh,
        in_specs=placed,
        out_specs=(P("dom", None), P("dom"), P(), P()),
        check_vma=False,
    )
```

profile of v0, /device:TPU:1, one launch (start us, length us, event | category | flops | bytes accessed | tf_op | source)
XLA Modules:
  0.0 614.2 jit_solution(8393531374904813304)
XLA Ops:
  8.5 3.3 collective-permute-start
  21.4 2.5 copy.31
  24.9 3.9 collective-permute-done.1
  28.8 1.7 broadcast_select_fusion.18
  32.5 6.8 %collective-permute-done.2 = bf16[256,400]{1,0:T(8,128)(2,1)} collective-permute-done((bf16[256,400]{1,0:T(8,128)(2,1)}, bf16[256,400]{1,0:T(8,128)(2,1)}, u32[]{:S(2)}, u32[]{:S(2)}) %collective-permute-start.2) | collective-permute-done | bytes 204832 | tf_op jit(solution)/shard_map/ppermute | solution.py:15
  40.4 6.1 collective-permute-done.3
  48.2 5.1 collective-permute-done.4
  53.5 5.2 collective-permute-done.5
  58.7 1.6 collective-permute-start.6
  61.0 9.9 %collective-permute-done.6 = bf16[256,400]{1,0:T(8,128)(2,1)S(1)} collective-permute-done((bf16[256,400]{1,0:T(8,128)(2,1)S(1)}, bf16[256,400]{1,0:T(8,128)(2,1)S(1)}, u32[]{:S(2)}, u32[]{:S(2)}) %collective-permute-start.6) | collective-permute-done | bytes 204832 | tf_op jit(solution)/shard_map/ppermute | solution.py:15
  71.0 2.2 collective-permute-start.7
  73.2 9.3 %collective-permute-done.7 = bf16[256,400]{1,0:T(8,128)(2,1)S(1)} collective-permute-done((bf16[256,400]{1,0:T(8,128)(2,1)S(1)}, bf16[256,400]{1,0:T(8,128)(2,1)S(1)}, u32[]{:S(2)}, u32[]{:S(2)}) %collective-permute-start.7) | collective-permute-done | bytes 204832 | tf_op jit(solution)/shard_map/ppermute | solution.py:15
  83.4 5.1 gather_fusion.3
  90.2 1.7 fusion.12
  92.0 1.8 fusion.28
  95.1 1.5 scatter_custom_fusion
  96.6 7.7 %scatter_fusion = f32[256,400]{1,0:T(8,128)S(1)} fusion(f32[256,400]{1,0:T(8,128)S(1)} %scatter_custom_fusion, s32[1000]{0:T(1024)S(1)} %bitcast.66, f32[1000,400]{1,0:T(8,128)} %fusion.28), kind=kCustom, calls=%fused_computation.9 | custom fusion | flops 400000 | bytes 4804000 | tf_op jit(solution)/shard_map/scatter-add | solution.py:58
  104.3 11.1 %collective-permute-start.8 = (bf16[256,400]{1,0:T(8,128)(2,1)S(1)}, bf16[256,400]{1,0:T(8,128)(2,1)S(1)}, u32[]{:S(2)}, u32[]{:S(2)}) collective-permute-start(bf16[256,400]{1,0:T(8,128)(2,1)S(1)} %convert_element_type.81), channel_id=1, source_target_pairs={{0,1},{1,0},{2,3},{3,2},{4,5},{5,4},{6,7},{7,6},{8,9},{9,8},{10,11... | collective-permute-start | bytes 614408 | tf_op jit(solution)/shard_map/ppermute | solution.py:15
  117.9 6.2 %collective-permute-done.9 = bf16[256,400]{1,0:T(8,128)(2,1)S(1)} collective-permute-done((bf16[256,400]{1,0:T(8,128)(2,1)S(1)}, bf16[256,400]{1,0:T(8,128)(2,1)S(1)}, u32[]{:S(2)}, u32[]{:S(2)}) %collective-permute-start.9) | collective-permute-done | bytes 204832 | tf_op jit(solution)/shard_map/ppermute | solution.py:15
  124.2 3.0 collective-permute-start.10
  127.2 5.2 collective-permute-done.10
  133.8 4.4 collective-permute-done.11
  138.2 2.9 collective-permute-start.12
  141.1 4.5 collective-permute-done.12
  145.8 5.2 collective-permute-done.13
  151.9 11.4 %collective-permute-done.14 = bf16[256,400]{1,0:T(8,128)(2,1)S(1)} collective-permute-done((bf16[256,400]{1,0:T(8,128)(2,1)S(1)}, bf16[256,400]{1,0:T(8,128)(2,1)S(1)}, u32[]{:S(2)}, u32[]{:S(2)}) %collective-permute-start.14) | collective-permute-done | bytes 204832 | tf_op jit(solution)/shard_map/ppermute | solution.py:15
  163.4 2.3 collective-permute-start.15
  165.9 13.4 %collective-permute-done.15 = bf16[256,400]{1,0:T(8,128)(2,1)} collective-permute-done((bf16[256,400]{1,0:T(8,128)(2,1)S(1)}, bf16[256,400]{1,0:T(8,128)(2,1)}, u32[]{:S(2)}, u32[]{:S(2)}) %collective-permute-start.15) | collective-permute-done | bytes 204832 | tf_op jit(solution)/shard_map/ppermute | solution.py:15
  180.1 3.2 scatter_fusion.1
  184.5 2.0 fusion.25
  186.5 1.8 collective-permute-start.16
  191.5 5.6 collective-permute-done.17
  197.1 3.0 collective-permute-start.18
  200.8 4.5 collective-permute-done.18
  205.3 4.4 collective-permute-start.19
  210.4 3.8 collective-permute-done.19
  214.3 4.8 collective-permute-start.20
  221.6 3.1 collective-permute-done.20
  228.2 3.0 collective-permute-done.21
  231.2 1.7 broadcast_select_fusion.11
  237.2 9.2 %collective-permute-done.22 = bf16[256,400]{1,0:T(8,128)(2,1)} collective-permute-done((bf16[256,400]{1,0:T(8,128)(2,1)}, bf16[256,400]{1,0:T(8,128)(2,1)}, u32[]{:S(2)}, u32[]{:S(2)}) %collective-permute-start.22) | collective-permute-done | bytes 204832 | tf_op jit(solution)/shard_map/ppermute | solution.py:15
  247.4 2.6 collective-permute-start.23
  250.8 13.9 %collective-permute-done.23 = bf16[256,400]{1,0:T(8,128)(2,1)} collective-permute-done((bf16[256,400]{1,0:T(8,128)(2,1)S(1)}, bf16[256,400]{1,0:T(8,128)(2,1)}, u32[]{:S(2)}, u32[]{:S(2)}) %collective-permute-start.23) | collective-permute-done | bytes 204832 | tf_op jit(solution)/shard_map/ppermute | solution.py:15
  265.8 1.5 gather_fusion.6
  267.3 1.6 copy.46
  270.6 5.1 gather_fusion.7
  275.7 1.7 fusion.13
  277.4 1.8 fusion.29
  281.2 1.9 scatter_custom_fusion.3
  283.1 7.5 %scatter_fusion.2 = f32[256,400]{1,0:T(8,128)S(1)} fusion(f32[256,400]{1,0:T(8,128)S(1)} %scatter_custom_fusion.3, s32[1000]{0:T(1024)S(1)} %bitcast.65, f32[1000,400]{1,0:T(8,128)} %fusion.29), kind=kCustom, calls=%fused_computation.12 | custom fusion | flops 400000 | bytes 4804000 | tf_op jit(solution)/shard_map/scatter-add | solution.py:58
  293.8 6.2 %collective-permute-done.25 = bf16[256,400]{1,0:T(8,128)(2,1)S(1)} collective-permute-done((bf16[256,400]{1,0:T(8,128)(2,1)S(1)}, bf16[256,400]{1,0:T(8,128)(2,1)S(1)}, u32[]{:S(2)}, u32[]{:S(2)}) %collective-permute-start.25) | collective-permute-done | bytes 204832 | tf_op jit(solution)/shard_map/ppermute | solution.py:15
  300.8 2.9 collective-permute-start.26
  304.8 4.3 scatter_custom_fusion.6
  310.5 5.7 collective-permute-done.27
  318.1 5.5 collective-permute-done.28
  325.0 244.6 %all-reduce.2.cloned.1.call-done = f32[1300,400]{1,0:T(8,128)} async-done(((f32[1300,400]{1,0:T(8,128)}), f32[1300,400]{1,0:T(8,128)}) %all-reduce.2.cloned.1.call-update) | async-done | bytes 2080016 | tf_op jit(solution)/shard_map/psum | solution.py:100
  569.6 2.2 multiply_reduce_fusion
  571.8 3.5 collective-permute-start.30
  575.9 10.7 %collective-permute-done.30 = bf16[256,400]{1,0:T(8,128)(2,1)S(1)} collective-permute-done((bf16[256,400]{1,0:T(8,128)(2,1)S(1)}, bf16[256,400]{1,0:T(8,128)(2,1)S(1)}, u32[]{:S(2)}, u32[]{:S(2)}) %collective-permute-start.30) | collective-permute-done | bytes 204832 | tf_op jit(solution)/shard_map/ppermute | solution.py:15
  586.6 4.0 collective-permute-start.31
  590.6 2.0 divide_subtract_fusion
  592.6 3.1 copy.54
  595.7 7.9 %collective-permute-done.31 = bf16[256,400]{1,0:T(8,128)(2,1)S(1)} collective-permute-done((bf16[256,400]{1,0:T(8,128)(2,1)S(1)}, bf16[256,400]{1,0:T(8,128)(2,1)S(1)}, u32[]{:S(2)}, u32[]{:S(2)}) %collective-permute-start.31) | collective-permute-done | bytes 204832 | tf_op jit(solution)/shard_map/ppermute | solution.py:15
  603.6 1.6 scatter_fusion.3
  (151 shorter events, 52.2 us)
Async XLA Ops:
  7.2 562.4 %all-reduce.2.cloned.1.call-start = ((), (), s32[]{:S(2)}) async-start(), calls=%async_computation | async-start | bytes 5341184 | tf_op jit(solution)/shard_map/psum | solution.py:100
  8.4 15.5 %copy-start = (f32[256,400]{1,0:T(8,128)}, f32[256,400]{1,0:T(8,128)S(1)}, u32[]{:S(2)}) copy-start(f32[256,400]{1,0:T(8,128)S(1)} %copy.40) | copy-start | bytes 1228804
  8.5 11.3 %collective-permute-start = (bf16[256,400]{1,0:T(8,128)(2,1)S(1)}, bf16[256,400]{1,0:T(8,128)(2,1)S(1)}, u32[]{:S(2)}, u32[]{:S(2)}) collective-permute-start(bf16[256,400]{1,0:T(8,128)(2,1)S(1)} %convert_element_type.78), channel_id=1, source_target_pairs={{0,1},{1,0},{2,3},{3,2},{4,5},{5,4},{6,7},{7,6},{8,9},{9,8},{10,11... | collective-permute-start | bytes 614408 | tf_op jit(solution)/shard_map/ppermute | solution.py:15
  20.5 8.2 %collective-permute-start.1 = (bf16[256,400]{1,0:T(8,128)(2,1)}, bf16[256,400]{1,0:T(8,128)(2,1)}, u32[]{:S(2)}, u32[]{:S(2)}) collective-permute-start(bf16[256,400]{1,0:T(8,128)(2,1)} %broadcast_select_fusion.16), channel_id=1, source_target_pairs={{0,2},{1,3},{2,0},{3,1},{4,6},{5,7},{6,4},{7,5},{8,10},{9,11},{10,... | collective-permute-start | bytes 614408 | tf_op jit(solution)/shard_map/ppermute | solution.py:15
  23.9 16.5 %copy-start.19 = (s32[2,128]{1,0:T(2,128)S(1)}, s32[2,128]{1,0:T(2,128)}, u32[]{:S(2)}) copy-start(s32[2,128]{1,0:T(2,128)} %param.17) | copy-start | bytes 3076
  24.0 23.7 %copy-start.18 = (s32[2,1]{0,1:T(1,128)S(1)}, s32[2,1]{0,1:T(1,128)}, u32[]{:S(2)}) copy-start(s32[2,1]{0,1:T(1,128)} %param.18) | copy-start | bytes 28
  24.7 28.8 %copy-start.15 = (s32[2,1,1000]{2,1,0:T(1,128)S(1)}, s32[2,1,1000]{2,1,0:T(1,128)}, u32[]{:S(2)}) copy-start(s32[2,1,1000]{2,1,0:T(1,128)} %param.19) | copy-start | bytes 24004
  24.9 46.1 %copy-start.7 = (f32[128,400]{0,1:T(8,128)}, f32[128,400]{0,1:T(8,128)S(1)}, u32[]{:S(2)}) copy-start(f32[128,400]{0,1:T(8,128)S(1)} %copy.33) | copy-start | bytes 614404
  30.5 8.9 %collective-permute-start.2 = (bf16[256,400]{1,0:T(8,128)(2,1)}, bf16[256,400]{1,0:T(8,128)(2,1)}, u32[]{:S(2)}, u32[]{:S(2)}) collective-permute-start(bf16[256,400]{1,0:T(8,128)(2,1)} %broadcast_select_fusion.18), channel_id=1, source_target_pairs={{0,4},{1,5},{2,6},{3,7},{4,0},{5,1},{6,2},{7,3},{8,12},{9,13},{10,... | collective-permute-start | bytes 614408 | tf_op jit(solution)/shard_map/ppermute | solution.py:15
  40.3 6.2 %collective-permute-start.3 = (bf16[256,400]{1,0:T(8,128)(2,1)S(1)}, bf16[256,400]{1,0:T(8,128)(2,1)S(1)}, u32[]{:S(2)}, u32[]{:S(2)}) collective-permute-start(bf16[256,400]{1,0:T(8,128)(2,1)S(1)} %broadcast_select_fusion.20), channel_id=1, source_target_pairs={{0,8},{1,9},{2,10},{3,11},{4,12},{5,13},{6,14},{7,15},{8,0},{9,1},... | collective-permute-start | bytes 614408 | tf_op jit(solution)/shard_map/ppermute | solution.py:15
  46.6 6.8 %collective-permute-start.4 = (bf16[256,400]{1,0:T(8,128)(2,1)S(1)}, bf16[256,400]{1,0:T(8,128)(2,1)S(1)}, u32[]{:S(2)}, u32[]{:S(2)}) collective-permute-start(bf16[256,400]{1,0:T(8,128)(2,1)S(1)} %broadcast_select_fusion.22), channel_id=1, source_target_pairs={{0,16},{1,17},{2,18},{3,19},{4,20},{5,21},{6,22},{7,23},{8,24},{9,... | collective-permute-start | bytes 614408 | tf_op jit(solution)/shard_map/ppermute | solution.py:15
  53.4 5.3 collective-permute-start.5
  58.7 12.2 %collective-permute-start.6 = (bf16[256,400]{1,0:T(8,128)(2,1)S(1)}, bf16[256,400]{1,0:T(8,128)(2,1)S(1)}, u32[]{:S(2)}, u32[]{:S(2)}) collective-permute-start(bf16[256,400]{1,0:T(8,128)(2,1)S(1)} %broadcast_select_fusion.26), channel_id=1, source_target_pairs={{0,64},{1,65},{2,66},{3,67},{4,68},{5,69},{6,70},{7,71},{8,72},{9,... | collective-permute-start | bytes 614408 | tf_op jit(solution)/shard_map/ppermute | solution.py:15
  71.0 11.5 %collective-permute-start.7 = (bf16[256,400]{1,0:T(8,128)(2,1)S(1)}, bf16[256,400]{1,0:T(8,128)(2,1)S(1)}, u32[]{:S(2)}, u32[]{:S(2)}) collective-permute-start(bf16[256,400]{1,0:T(8,128)(2,1)S(1)} %broadcast_select_fusion.28), channel_id=1, source_target_pairs={{0,128},{1,129},{2,130},{3,131},{4,132},{5,133},{6,134},{7,135},{8... | collective-permute-start | bytes 614408 | tf_op jit(solution)/shard_map/ppermute | solution.py:15
  90.2 3.5 copy-start.5
  104.3 61.5 %copy-start.8 = (f32[128,400]{0,1:T(8,128)S(1)}, f32[128,400]{0,1:T(8,128)}, u32[]{:S(2)}) copy-start(f32[128,400]{0,1:T(8,128)} %copy-done.7) | copy-start | bytes 614404
  104.3 61.5 %copy-start.13 = (bf16[128,400]{0,1:T(8,128)(2,1)S(1)}, bf16[128,400]{0,1:T(8,128)(2,1)}, u32[]{:S(2)}) copy-start(bf16[128,400]{0,1:T(8,128)(2,1)} %get-tuple-element.15) | copy-start | bytes 307204
  104.3 12.2 %collective-permute-start.8 = (bf16[256,400]{1,0:T(8,128)(2,1)S(1)}, bf16[256,400]{1,0:T(8,128)(2,1)S(1)}, u32[]{:S(2)}, u32[]{:S(2)}) collective-permute-start(bf16[256,400]{1,0:T(8,128)(2,1)S(1)} %convert_element_type.81), channel_id=1, source_target_pairs={{0,1},{1,0},{2,3},{3,2},{4,5},{5,4},{6,7},{7,6},{8,9},{9,8},{10,11... | collective-permute-start | bytes 614408 | tf_op jit(solution)/shard_map/ppermute | solution.py:15
  116.6 7.6 %collective-permute-start.9 = (bf16[256,400]{1,0:T(8,128)(2,1)S(1)}, bf16[256,400]{1,0:T(8,128)(2,1)S(1)}, u32[]{:S(2)}, u32[]{:S(2)}) collective-permute-start(bf16[256,400]{1,0:T(8,128)(2,1)S(1)} %broadcast_select_fusion.15), channel_id=1, source_target_pairs={{0,2},{1,3},{2,0},{3,1},{4,6},{5,7},{6,4},{7,5},{8,10},{9,11},{10,... | collective-permute-start | bytes 614408 | tf_op jit(solution)/shard_map/ppermute | solution.py:15
  124.2 8.2 %collective-permute-start.10 = (bf16[256,400]{1,0:T(8,128)(2,1)S(1)}, bf16[256,400]{1,0:T(8,128)(2,1)S(1)}, u32[]{:S(2)}, u32[]{:S(2)}) collective-permute-start(bf16[256,400]{1,0:T(8,128)(2,1)S(1)} %broadcast_select_fusion.17), channel_id=1, source_target_pairs={{0,4},{1,5},{2,6},{3,7},{4,0},{5,1},{6,2},{7,3},{8,12},{9,13},{10,... | collective-permute-start | bytes 614408 | tf_op jit(solution)/shard_map/ppermute | solution.py:15
  132.4 5.8 collective-permute-start.11
  138.2 7.4 %collective-permute-start.12 = (bf16[256,400]{1,0:T(8,128)(2,1)S(1)}, bf16[256,400]{1,0:T(8,128)(2,1)S(1)}, u32[]{:S(2)}, u32[]{:S(2)}) collective-permute-start(bf16[256,400]{1,0:T(8,128)(2,1)S(1)} %broadcast_select_fusion.21), channel_id=1, source_target_pairs={{0,16},{1,17},{2,18},{3,19},{4,20},{5,21},{6,22},{7,23},{8,24},{9,... | collective-permute-start | bytes 614408 | tf_op jit(solution)/shard_map/ppermute | solution.py:15
  145.7 5.3 collective-permute-start.13
  151.0 12.4 %collective-permute-start.14 = (bf16[256,400]{1,0:T(8,128)(2,1)S(1)}, bf16[256,400]{1,0:T(8,128)(2,1)S(1)}, u32[]{:S(2)}, u32[]{:S(2)}) collective-permute-start(bf16[256,400]{1,0:T(8,128)(2,1)S(1)} %broadcast_select_fusion.25), channel_id=1, source_target_pairs={{0,64},{1,65},{2,66},{3,67},{4,68},{5,69},{6,70},{7,71},{8,72},{9,... | collective-permute-start | bytes 614408 | tf_op jit(solution)/shard_map/ppermute | solution.py:15
  163.4 15.9 %collective-permute-start.15 = (bf16[256,400]{1,0:T(8,128)(2,1)S(1)}, bf16[256,400]{1,0:T(8,128)(2,1)}, u32[]{:S(2)}, u32[]{:S(2)}) collective-permute-start(bf16[256,400]{1,0:T(8,128)(2,1)S(1)} %broadcast_select_fusion.27), channel_id=1, source_target_pairs={{0,128},{1,129},{2,130},{3,131},{4,132},{5,133},{6,134},{7,135},{8... | collective-permute-start | bytes 614408 | tf_op jit(solution)/shard_map/ppermute | solution.py:15
  180.1 4.3 copy-start.17
  180.1 4.4 copy-start.1
  186.5 3.0 collective-permute-start.16
  189.4 7.6 %collective-permute-start.17 = (bf16[256,400]{1,0:T(8,128)(2,1)S(1)}, bf16[256,400]{1,0:T(8,128)(2,1)S(1)}, u32[]{:S(2)}, u32[]{:S(2)}) collective-permute-start(bf16[256,400]{1,0:T(8,128)(2,1)S(1)} %broadcast_select_fusion.1), channel_id=1, source_target_pairs={{0,2},{1,3},{2,0},{3,1},{4,6},{5,7},{6,4},{7,5},{8,10},{9,11},{10,... | collective-permute-start | bytes 614408 | tf_op jit(solution)/shard_map/ppermute | solution.py:15
  197.1 8.2 %collective-permute-start.18 = (bf16[256,400]{1,0:T(8,128)(2,1)S(1)}, bf16[256,400]{1,0:T(8,128)(2,1)S(1)}, u32[]{:S(2)}, u32[]{:S(2)}) collective-permute-start(bf16[256,400]{1,0:T(8,128)(2,1)S(1)} %broadcast_select_fusion.3), channel_id=1, source_target_pairs={{0,4},{1,5},{2,6},{3,7},{4,0},{5,1},{6,2},{7,3},{8,12},{9,13},{10,... | collective-permute-start | bytes 614408 | tf_op jit(solution)/shard_map/ppermute | solution.py:15
  205.3 29.4 %copy-start.2 = (f32[256,400]{1,0:T(8,128)S(1)}, f32[256,400]{1,0:T(8,128)}, u32[]{:S(2)}) copy-start(f32[256,400]{1,0:T(8,128)} %get-tuple-element.21) | copy-start | bytes 1228804
  205.3 8.9 %collective-permute-start.19 = (bf16[256,400]{1,0:T(8,128)(2,1)S(1)}, bf16[256,400]{1,0:T(8,128)(2,1)S(1)}, u32[]{:S(2)}, u32[]{:S(2)}) collective-permute-start(bf16[256,400]{1,0:T(8,128)(2,1)S(1)} %broadcast_select_fusion.5), channel_id=1, source_target_pairs={{0,8},{1,9},{2,10},{3,11},{4,12},{5,13},{6,14},{7,15},{8,0},{9,1},... | collective-permute-start | bytes 614408 | tf_op jit(solution)/shard_map/ppermute | solution.py:15
  214.3 10.4 %collective-permute-start.20 = (bf16[256,400]{1,0:T(8,128)(2,1)S(1)}, bf16[256,400]{1,0:T(8,128)(2,1)S(1)}, u32[]{:S(2)}, u32[]{:S(2)}) collective-permute-start(bf16[256,400]{1,0:T(8,128)(2,1)S(1)} %broadcast_select_fusion.7), channel_id=1, source_target_pairs={{0,16},{1,17},{2,18},{3,19},{4,20},{5,21},{6,22},{7,23},{8,24},{9,... | collective-permute-start | bytes 614408 | tf_op jit(solution)/shard_map/ppermute | solution.py:15
  225.4 5.7 collective-permute-start.21
  232.8 13.6 %collective-permute-start.22 = (bf16[256,400]{1,0:T(8,128)(2,1)}, bf16[256,400]{1,0:T(8,128)(2,1)}, u32[]{:S(2)}, u32[]{:S(2)}) collective-permute-start(bf16[256,400]{1,0:T(8,128)(2,1)} %broadcast_select_fusion.11), channel_id=1, source_target_pairs={{0,64},{1,65},{2,66},{3,67},{4,68},{5,69},{6,70},{7,71},{8,72},{9,... | collective-permute-start | bytes 614408 | tf_op jit(solution)/shard_map/ppermute | solution.py:15
  247.4 17.4 %copy-start.9 = (bf16[256,400]{1,0:T(8,128)(2,1)}, bf16[256,400]{1,0:T(8,128)(2,1)S(1)}, u32[]{:S(2)}) copy-start(bf16[256,400]{1,0:T(8,128)(2,1)S(1)} %broadcast_select_fusion.13) | copy-start | bytes 614404
  247.4 17.3 %collective-permute-start.23 = (bf16[256,400]{1,0:T(8,128)(2,1)S(1)}, bf16[256,400]{1,0:T(8,128)(2,1)}, u32[]{:S(2)}, u32[]{:S(2)}) collective-permute-start(bf16[256,400]{1,0:T(8,128)(2,1)S(1)} %broadcast_select_fusion.13), channel_id=1, source_target_pairs={{0,128},{1,129},{2,130},{3,131},{4,132},{5,133},{6,134},{7,135},{8... | collective-permute-start | bytes 614408 | tf_op jit(solution)/shard_map/ppermute | solution.py:15
  275.6 3.5 copy-start.6
  275.6 3.5 copy-start.12
  290.6 13.1 %copy-start.10 = (f32[128,400]{0,1:T(8,128)S(1)}, f32[128,400]{0,1:T(8,128)}, u32[]{:S(2)}) copy-start(f32[128,400]{0,1:T(8,128)} %get-tuple-element.14) | copy-start | bytes 614404
  290.6 13.1 %copy-start.11 = (f32[128,400]{0,1:T(8,128)S(1)}, f32[128,400]{0,1:T(8,128)}, u32[]{:S(2)}) copy-start(f32[128,400]{0,1:T(8,128)} %get-tuple-element.16) | copy-start | bytes 614404
  290.6 1.7 collective-permute-start.24
  292.4 7.6 %collective-permute-start.25 = (bf16[256,400]{1,0:T(8,128)(2,1)S(1)}, bf16[256,400]{1,0:T(8,128)(2,1)S(1)}, u32[]{:S(2)}, u32[]{:S(2)}) collective-permute-start(bf16[256,400]{1,0:T(8,128)(2,1)S(1)} %broadcast_select_fusion), channel_id=1, source_target_pairs={{0,2},{1,3},{2,0},{3,1},{4,6},{5,7},{6,4},{7,5},{8,10},{9,11},{10,... | collective-permute-start | bytes 614408 | tf_op jit(solution)/shard_map/ppermute | solution.py:15
  300.8 8.4 %collective-permute-start.26 = (bf16[256,400]{1,0:T(8,128)(2,1)}, bf16[256,400]{1,0:T(8,128)(2,1)}, u32[]{:S(2)}, u32[]{:S(2)}) collective-permute-start(bf16[256,400]{1,0:T(8,128)(2,1)} %broadcast_select_fusion.2), channel_id=1, source_target_pairs={{0,4},{1,5},{2,6},{3,7},{4,0},{5,1},{6,2},{7,3},{8,12},{9,13},{10,... | collective-permute-start | bytes 614408 | tf_op jit(solution)/shard_map/ppermute | solution.py:15
  309.0 7.3 %copy-start.14 = (bf16[128,400]{0,1:T(8,128)(2,1)S(1)}, bf16[128,400]{0,1:T(8,128)(2,1)}, u32[]{:S(2)}) copy-start(bf16[128,400]{0,1:T(8,128)(2,1)} %get-tuple-element.17) | copy-start | bytes 307204
  310.2 6.0 collective-permute-start.27
  316.2 259.1 %copy-start.16 = (f32[1300]{0:T(1024)S(1)}, f32[1300]{0:T(1024)}, u32[]{:S(2)}) copy-start(f32[1300]{0:T(1024)} %param.13) | copy-start | bytes 15604
  316.2 7.4 %collective-permute-start.28 = (bf16[256,400]{1,0:T(8,128)(2,1)S(1)}, bf16[256,400]{1,0:T(8,128)(2,1)}, u32[]{:S(2)}, u32[]{:S(2)}) collective-permute-start(bf16[256,400]{1,0:T(8,128)(2,1)S(1)} %broadcast_select_fusion.6), channel_id=1, source_target_pairs={{0,16},{1,17},{2,18},{3,19},{4,20},{5,21},{6,22},{7,23},{8,24},{9,... | collective-permute-start | bytes 614408 | tf_op jit(solution)/shard_map/ppermute | solution.py:15
  324.6 247.2 %collective-permute-start.29 = (bf16[256,400]{1,0:T(8,128)(2,1)S(1)}, bf16[256,400]{1,0:T(8,128)(2,1)S(1)}, u32[]{:S(2)}, u32[]{:S(2)}) collective-permute-start(bf16[256,400]{1,0:T(8,128)(2,1)S(1)} %broadcast_select_fusion.8), channel_id=1, source_target_pairs={{0,32},{1,33},{2,34},{3,35},{4,36},{5,37},{6,38},{7,39},{8,40},{9,... | collective-permute-start | bytes 614408 | tf_op jit(solution)/shard_map/ppermute | solution.py:15
  569.6 21.0 %copy-start.4 = (f32[1300,400]{1,0:T(8,128)S(1)}, f32[1300,400]{1,0:T(8,128)}, u32[]{:S(2)}) copy-start(f32[1300,400]{1,0:T(8,128)} %all-reduce.2.cloned.1.call-done) | copy-start | bytes 6240004
  571.8 14.8 %collective-permute-start.30 = (bf16[256,400]{1,0:T(8,128)(2,1)S(1)}, bf16[256,400]{1,0:T(8,128)(2,1)S(1)}, u32[]{:S(2)}, u32[]{:S(2)}) collective-permute-start(bf16[256,400]{1,0:T(8,128)(2,1)S(1)} %broadcast_select_fusion.10), channel_id=1, source_target_pairs={{0,64},{1,65},{2,66},{3,67},{4,68},{5,69},{6,70},{7,71},{8,72},{9,... | collective-permute-start | bytes 614408 | tf_op jit(solution)/shard_map/ppermute | solution.py:15
  586.6 17.0 %collective-permute-start.31 = (bf16[256,400]{1,0:T(8,128)(2,1)S(1)}, bf16[256,400]{1,0:T(8,128)(2,1)S(1)}, u32[]{:S(2)}, u32[]{:S(2)}) collective-permute-start(bf16[256,400]{1,0:T(8,128)(2,1)S(1)} %broadcast_select_fusion.12), channel_id=1, source_target_pairs={{0,128},{1,129},{2,130},{3,131},{4,132},{5,133},{6,134},{7,135},{8... | collective-permute-start | bytes 614408 | tf_op jit(solution)/shard_map/ppermute | solution.py:15
  603.6 2.3 copy-start.3
Sparse Core Ops, SparseCore 0:
  309.2 260.3 all-reduce.1
where the time goes:
time: 623 us; the launch traced here: 614 us
  waiting for transfers between devices  423 us (68%)
  starting transfers between devices  65.3 us (10%)
  other arithmetic  55.3 us (9%)
  local copies, waits for them, and re-layouts  35.5 us (6%)
  between operations  25.5 us (4%)
  matrix products  9.42 us (2%)
    psum x1, waiting for transfers between devices, shards(): rel_total = lax.psum(rel_total, 'dom')  245 us
    ppermute x32, waiting for transfers between devices, from_partner(): return lax.ppermute(value, axis, pairs)  179 us
    ppermute x32, starting transfers between devices, from_partner(): return lax.ppermute(value, axis, pairs)  65.2 us
    scatter-add x2, other arithmetic, bucket_grads(): dest_grads = dest_grads.at[neg_ids.reshape(-1)].add(row_terms)  15.1 us
  transfers between devices with their start and end apart: 33, of which 31 were waited for; matrix products, arithmetic and copies ran while one was open for 5% of the time, Pallas kernels for 0%

commit v1 on v0

v1 whole, which is shorter than its diff:
```python
import jax
import jax.numpy as jnp
from jax import lax
from jax.experimental import pallas as pl
from jax.experimental.pallas import tpu as pltpu
from jax.sharding import PartitionSpec as P

ROUNDS = 2
D = 400
NREL = 1300
NEG = 1000
ROWS = 256
EDGES = 128
WIDE = 512
LEFT = D - 384
TILES = 32
BLOCK = 1304
GROUP = 168
PACKED = 4096

learning_rate = 0.1

F32 = jnp.float32
BF16 = jnp.bfloat16


def iota(shape, dim):
    return lax.broadcasted_iota(jnp.int32, shape, dim)


def dot(a, b, left=1, right=0):
    return lax.dot_general(a, b, (((left,), (right,)), ((), ())), preferred_element_type=F32)


def halves(value):
    high = value.astype(BF16)
    return high, (value - high.astype(F32)).astype(BF16)


def as_column(row):
    count = row.shape[1]
    square = (count, count)
    return jnp.sum(jnp.where(iota(square, 0) == iota(square, 1), row, 0.0), axis=1, keepdims=True)


def as_row(column):
    count = column.shape[0]
    square = (count, count)
    return jnp.sum(jnp.where(iota(square, 0) == iota(square, 1), column, 0.0), axis=0, keepdims=True)


def remote(source, target, send, recv, device):
    return pltpu.make_async_remote_copy(
        src_ref=source,
        dst_ref=target,
        send_sem=send,
        recv_sem=recv,
        device_id=(device,),
        device_id_type=pl.DeviceIdType.MESH,
    )


def await_bytes(ref, sem):
    pltpu.make_async_copy(ref, ref, sem).wait()


def kernel(
    masks,
    src_ids,
    rel_ids,
    counts,
    emb_in,
    state_in,
    relations,
    rel_state_in,
    src_rows,
    rel_rows,
    dst_rows,
    neg_rows,
    emb_out,
    state_out,
    rel_out,
    rel_state_out,
    emb,
    srcs,
    rels,
    block,
    dest,
    grads,
    packed,
    state_col,
    x1,
    b1,
    x2,
    b2,
    x3,
    b3,
    t0,
    r0,
    t1,
    ra,
    t2,
    rb,
    t3,
    rz,
    gathered,
    send,
    recv,
    sum_send,
    sum_recv,
):
    me = lax.axis_index("dom")
    a = me // 8
    b = me % 8
    c = me % 2
    y = (me // 2) % 4
    x = (me // 8) % 4
    z = me // 32

    barrier = pltpu.get_barrier_semaphore()

    def tell(device):
        pl.semaphore_signal(barrier, inc=1, device_id=(device,), device_id_type=pl.DeviceIdType.MESH)

    def tell_a(step, _):
        tell(((a + step) % 32) * 8 + b)
        return 0

    def tell_b(step, _):
        tell(a * 8 + (b + step) % 8)
        return 0

    def tell_c(step, _):
        device = ((a + step) % 32) * 8 + a % 8

        @pl.when(device != me)
        def _():
            tell(device)

        return 0

    lax.fori_loop(1, 32, tell_a, 0)
    lax.fori_loop(1, 8, tell_b, 0)
    lax.fori_loop(0, 32, tell_c, 0)

    def gather_rels(r):
        rels[r, :, 384:] = jnp.zeros((EDGES, 128), F32)
        for e in range(EDGES):
            rels[r, e : e + 1, :D] = relations[pl.ds(rel_ids[r, e], 1), :]

    def gather_srcs(r):
        for e in range(EDGES):
            srcs[r, e : e + 1, :] = emb[pl.ds(src_ids[r, e], 1), :]

    def vectors_out(r):
        values = srcs[r] * rels[r]
        dst = as_column(dst_rows[r : r + 1, :].astype(F32))
        live = (iota((EDGES, 1), 0) < counts[r, 0]).astype(F32)
        negatives = neg_rows[r : r + 1, :]
        hits = jnp.sum((iota((ROWS, NEG), 0) == negatives).astype(F32), axis=1, keepdims=True)
        high = jnp.floor(hits * (1.0 / 16.0))
        low = hits - 16.0 * high
        lane = iota((EDGES, 128), 1)
        last = values[:, 384:]
        extras = (dst, live, high[:128], high[128:], low[:128], low[128:])
        for n, extra in enumerate(extras):
            last = jnp.where(lane == LEFT + n, extra, last)
        put_block(2 * r, values[:, :384].astype(BF16), last.astype(BF16))

    def put_block(k, main, last):
        for i in range(8):
            for j in range(4):
                part = main[16 * i : 16 * i + 16, 128 * j : 128 * j + 128] if j < 3 else last[16 * i : 16 * i + 16]
                x1[k, 4 * i + j] = part

    def exchange(k, mask, during=None):
        mask_a = lax.shift_right_logical(mask, 3)
        mask_b = lax.bitwise_and(mask, 7)

        def first(step, _):
            t = (a + step) % 32
            remote(x1.at[k, t], b1.at[k, a], send.at[k, 0], recv.at[k, 0], t * 8 + b).start()
            return 0

        lax.fori_loop(1, 32, first, 0)
        b1[k, a] = x1[k, a]
        if during is not None:
            during()
        await_bytes(b1.at[k, pl.ds(0, 31)], recv.at[k, 0])

        for low in range(8):
            for h in range(4):
                x2[k, 4 * low + h] = b1[k, lax.bitwise_xor(mask_a, 8 * h + low)]

        def second(step, _):
            to = (b + step) % 8
            remote(
                x2.at[k, pl.ds(4 * to, 4)],
                b2.at[k, pl.ds(4 * b, 4)],
                send.at[k, 1],
                recv.at[k, 1],
                a * 8 + to,
            ).start()
            return 0

        lax.fori_loop(1, 8, second, 0)
        b2[k, pl.ds(4 * b, 4)] = x2[k, pl.ds(4 * b, 4)]
        await_bytes(b2.at[k, pl.ds(0, 28)], recv.at[k, 1])

        for to in range(8):
            from_b = lax.bitwise_xor(mask_b, to)
            x3[k, 4 * to : 4 * to + 4] = b2[k, pl.ds(4 * from_b, 4)]

        def third(step, _):
            n = (a + step) % 32
            h = n // 8
            to = n % 8
            device = (8 * h + b) * 8 + to

            @pl.when(device != me)
            def _():
                remote(x3.at[k, 4 * to + h], b3.at[k, a], send.at[k, 2], recv.at[k, 2], device).start()

            @pl.when(device == me)
            def _():
                b3[k, a] = x3[k, 4 * to + h]

            return 0

        lax.fori_loop(0, 32, third, 0)

        @pl.when(a % 8 == b)
        def _():
            await_bytes(b3.at[k, pl.ds(0, 31)], recv.at[k, 2])

        @pl.when(a % 8 != b)
        def _():
            await_bytes(b3.at[k], recv.at[k, 2])

        for i in range(8):
            for j in range(4):
                block[16 * i : 16 * i + 16, 128 * j : 128 * j + 128] = b3[k, 4 * i + j]

    def sent(k):
        await_bytes(x1.at[k, pl.ds(0, 31)], send.at[k, 0])
        await_bytes(x2.at[k, pl.ds(0, 28)], send.at[k, 1])

        @pl.when(a % 8 == b)
        def _():
            await_bytes(x3.at[k, pl.ds(0, 31)], send.at[k, 2])

        @pl.when(a % 8 != b)
        def _():
            await_bytes(x3.at[k], send.at[k, 2])

    emb[:, 384:] = jnp.zeros((ROWS, 128), F32)
    emb[:, :D] = emb_in[...]
    gather_rels(0)
    gather_srcs(0)
    vectors_out(0)
    state = jnp.concatenate([as_column(state_in[:, :128]), as_column(state_in[:, 128:])], axis=0)
    for n in range(11):
        width = min(128, NREL - 128 * n)
        part = rel_state_in[:, 128 * n : 128 * n + width]
        if width < 128:
            part = jnp.concatenate([part, jnp.ones((1, 128 - width), F32)], axis=1)
        state_col[128 * n : 128 * n + 128, :] = as_column(part)

    @pl.when(a % 8 == b)
    def _():
        pl.semaphore_wait(barrier, 31 + 7 + 31)

    @pl.when(a % 8 != b)
    def _():
        pl.semaphore_wait(barrier, 31 + 7 + 32)

    for r in range(ROUNDS):
        mask = masks[r]
        exchange(2 * r, mask, (lambda: gather_rels(1)) if r == 0 else None)

        vec = block[...]
        table = emb[...].astype(BF16)
        scores = dot(vec, table, 1, 1)
        meta = vec[:, 384:].astype(F32)
        dst = meta[:, LEFT : LEFT + 1]
        live = meta[:, LEFT + 1 : LEFT + 2]
        hits = [
            as_row(16.0 * meta[:, LEFT + 2 + n : LEFT + 3 + n] + meta[:, LEFT + 4 + n : LEFT + 5 + n])
            for n in range(2)
        ]
        hits = jnp.concatenate(hits, axis=1)
        is_dst = iota((EDGES, ROWS), 1).astype(F32) == dst
        neg_coef = (live * (1.0 / (1.0 + jnp.exp(-scores))) / NEG).astype(BF16).astype(F32)
        positive = jnp.sum(jnp.where(is_dst, scores, 0.0), axis=1, keepdims=True)
        pos_coef = -live * (1.0 / (1.0 + jnp.exp(positive)))
        coef = neg_coef * hits + jnp.where(is_dst, pos_coef, 0.0)
        coef_high, coef_low = halves(coef)
        pulled = (dot(coef_high, table) + dot(coef_low, table)).astype(BF16)
        put_block(2 * r + 1, pulled[:, :384], pulled[:, 384:])

        def dest_part(vec=vec, coef_high=coef_high, coef_low=coef_low):
            total = dot(coef_high, vec, 0, 0) + dot(coef_low, vec, 0, 0)
            total = total.astype(BF16).astype(F32)
            dest[...] = jnp.where(iota((ROWS, WIDE), 1) < D, total, 0.0)

        exchange(2 * r + 1, mask, dest_part)

        wide = block[...].astype(F32)
        grads[r * EDGES : (r + 1) * EDGES, :] = wide * srcs[r]
        is_src = (iota((ROWS, EDGES), 0) == src_rows[r : r + 1, :]).astype(BF16)
        high, low = halves(wide * rels[r])
        grad = dest[...] + dot(is_src, high) + dot(is_src, low)
        state = state + jnp.sum(grad * grad, axis=1, keepdims=True) * (1.0 / D)
        emb[...] = emb[...] - learning_rate * grad / jnp.sqrt(state)
        if r + 1 < ROUNDS:
            gather_srcs(r + 1)
            vectors_out(r + 1)

    high, low = halves(grads[...])
    ids = jnp.concatenate([rel_rows[0:1, :], rel_rows[1:2, :]], axis=1)
    tail = jnp.zeros((GROUP, 128), F32)
    for g in range(8):
        rows = min(GROUP, BLOCK - GROUP * g)
        is_rel = (iota((GROUP, ROUNDS * EDGES), 0) + GROUP * g == ids).astype(BF16)
        part = dot(is_rel, high) + dot(is_rel, low)
        for n in range(3):
            at = BLOCK * n + GROUP * g
            packed[at : at + rows, :] = part[:rows, 128 * n : 128 * n + 128]
        end = part[:, 384:]
        tail = tail + (pltpu.roll(end, LEFT * g, 1) if g else end)
    packed[3 * BLOCK : 3 * BLOCK + GROUP, :] = tail
    packed[3 * BLOCK + GROUP :, :] = jnp.zeros((PACKED - 3 * BLOCK - GROUP, 128), F32)
    t0[...] = packed[...].reshape(256, 16, 128).astype(BF16)

    def at_x(to):
        return ((z * 4 + to) * 4 + y) * 2 + c

    def at_y(to):
        return ((z * 4 + x) * 4 + to) * 2 + c

    def at_z(to):
        return ((to * 4 + x) * 4 + y) * 2 + c

    other = me + 1 - 2 * c

    remote(t0.at[pl.ds((1 - c) * 128, 128)], r0, sum_send.at[0], sum_recv.at[0], other).start()
    await_bytes(r0, sum_recv.at[0])
    t1[...] = (t0[pl.ds(c * 128, 128)].astype(F32) + r0[...].astype(F32)).astype(BF16)

    for step in range(1, 4):
        to_x, to_y = (x + step) % 4, (y + step) % 4
        remote(t1.at[pl.ds(16 * to_x, 16)], ra.at[0, x], sum_send.at[1], sum_recv.at[1], at_x(to_x)).start()
        remote(t1.at[pl.ds(64 + 16 * to_y, 16)], ra.at[1, y], sum_send.at[2], sum_recv.at[2], at_y(to_y)).start()
    ra[0, x] = t1[pl.ds(16 * x, 16)]
    ra[1, y] = t1[pl.ds(64 + 16 * y, 16)]

    def added(ref, lead, count):
        total = ref[lead + (0,)].astype(F32)
        for n in range(1, count):
            total = total + ref[lead + (n,)].astype(F32)
        return total.astype(BF16)

    await_bytes(ra.at[0, pl.ds(0, 3)], sum_recv.at[1])
    t2[0] = added(ra, (0,), 4)
    for step in range(1, 4):
        to_y = (y + step) % 4
        remote(t2.at[0, pl.ds(4 * to_y, 4)], rb.at[0, y], sum_send.at[3], sum_recv.at[3], at_y(to_y)).start()
    rb[0, y] = t2[0, pl.ds(4 * y, 4)]
    await_bytes(ra.at[1, pl.ds(0, 3)], sum_recv.at[2])
    t2[1] = added(ra, (1,), 4)
    for step in range(1, 4):
        to_x = (x + step) % 4
        remote(t2.at[1, pl.ds(4 * to_x, 4)], rb.at[1, x], sum_send.at[4], sum_recv.at[4], at_x(to_x)).start()
    rb[1, x] = t2[1, pl.ds(4 * x, 4)]
    await_bytes(rb.at[0, pl.ds(0, 3)], sum_recv.at[3])
    t3[0:4] = added(rb, (0,), 4)
    await_bytes(rb.at[1, pl.ds(0, 3)], sum_recv.at[4])
    t3[4:8] = added(rb, (1,), 4)

    def spread_z(step, _):
        to = (z + step) % 8
        remote(t3.at[to], rz.at[z], sum_send.at[5], sum_recv.at[5], at_z(to)).start()
        return 0

    lax.fori_loop(1, 8, spread_z, 0)
    rz[z] = t3[z]
    await_bytes(rz.at[pl.ds(0, 7)], sum_recv.at[5])

    which = z // 4
    base_x = c * 128 + 16 * x + 4 * y
    base_y = c * 128 + 64 + 16 * y + 4 * x
    mine = (1 - which) * base_x + which * base_y + z % 4
    gathered[mine] = added(rz, (), 8)

    def gather_z(step, _):
        to = (z + step) % 8
        remote(gathered.at[mine], gathered.at[mine], sum_send.at[6], sum_recv.at[6], at_z(to)).start()
        return 0

    lax.fori_loop(1, 8, gather_z, 0)
    await_bytes(gathered.at[pl.ds(0, 7)], sum_recv.at[6])

    def whole(first, count, n, device):
        part = gathered.at[pl.ds(first, count)]
        return remote(part, part, sum_send.at[n], sum_recv.at[n], device)

    for step in range(1, 4):
        to_x, to_y = (x + step) % 4, (y + step) % 4
        whole(base_x, 4, 7, at_y(to_y)).start()
        whole(base_y, 4, 8, at_x(to_x)).start()
    await_bytes(gathered.at[pl.ds(0, 12)], sum_recv.at[7])
    await_bytes(gathered.at[pl.ds(0, 12)], sum_recv.at[8])
    for step in range(1, 4):
        to_x, to_y = (x + step) % 4, (y + step) % 4
        whole(c * 128 + 16 * x, 16, 9, at_x(to_x)).start()
        whole(c * 128 + 64 + 16 * y, 16, 10, at_y(to_y)).start()
    await_bytes(gathered.at[pl.ds(0, 48)], sum_recv.at[9])
    await_bytes(gathered.at[pl.ds(0, 48)], sum_recv.at[10])
    whole(c * 128, 128, 11, other).start()
    emb_out[...] = emb[:, :D]
    state_out[...] = jnp.concatenate([as_row(state[:128]), as_row(state[128:])], axis=1)
    await_bytes(gathered.at[pl.ds(0, 128)], sum_recv.at[11])

    packed[...] = gathered[...].astype(F32).reshape(PACKED, 128)
    for g in range(8):
        rows = min(GROUP, NREL - GROUP * g)
        at = GROUP * g
        parts = [packed[BLOCK * n + at : BLOCK * n + at + rows, :] for n in range(3)]
        end = packed[3 * BLOCK : 3 * BLOCK + GROUP, :]
        end = (pltpu.roll(end, 128 - LEFT * g, 1) if g else end)[:rows, :LEFT]
        squares = parts[0] * parts[0] + parts[1] * parts[1] + parts[2] * parts[2]
        mean = jnp.sum(squares, axis=1, keepdims=True) + jnp.sum(end * end, axis=1, keepdims=True)
        fresh = state_col[at : at + rows, :] + mean * (1.0 / D)
        state_col[at : at + rows, :] = fresh
        root = jnp.sqrt(fresh)
        for n in range(3):
            cols = slice(128 * n, 128 * n + 128)
            rel_out[at : at + rows, cols] = relations[at : at + rows, cols] - learning_rate * parts[n] / root
        rel_out[at : at + rows, 384:] = relations[at : at + rows, 384:] - learning_rate * end / root
    for n in range(11):
        width = min(128, NREL - 128 * n)
        row = as_row(state_col[128 * n : 128 * n + 128, :])
        rel_state_out[:, 128 * n : 128 * n + width] = row[:, :width]

    for k in range(2 * ROUNDS):
        sent(k)
    await_bytes(t0.at[pl.ds(0, 128)], sum_send.at[0])
    for n, tiles in ((1, 48), (2, 48), (3, 12), (4, 12), (5, 7), (6, 7), (7, 12), (8, 12), (9, 48), (10, 48), (11, 128)):
        await_bytes(gathered.at[pl.ds(0, tiles)], sum_send.at[n])


def shards(
    embeddings,
    entity_state,
    relations,
    relation_state,
    round_masks,
    edge_src,
    edge_rel,
    edge_dst,
    edge_count,
    neg_rows,
):
    smem = pl.BlockSpec(memory_space=pltpu.SMEM)
    vmem = pl.BlockSpec(memory_space=pltpu.VMEM)

    def tiles(*lead):
        return pltpu.VMEM(lead + (16, 128), BF16)

    new_rows, new_state, new_relations, new_relation_state = pl.pallas_call(
        kernel,
        out_shape=(
            jax.ShapeDtypeStruct((ROWS, D), F32),
            jax.ShapeDtypeStruct((1, ROWS), F32),
            jax.ShapeDtypeStruct((NREL, D), F32),
            jax.ShapeDtypeStruct((1, NREL), F32),
        ),
        in_specs=[smem] * 4 + [vmem] * 8,
        out_specs=(vmem,) * 4,
        scratch_shapes=[
            pltpu.VMEM((ROWS, WIDE), F32),
            pltpu.VMEM((ROUNDS, EDGES, WIDE), F32),
            pltpu.VMEM((ROUNDS, EDGES, WIDE), F32),
            pltpu.VMEM((EDGES, WIDE), BF16),
            pltpu.VMEM((ROWS, WIDE), F32),
            pltpu.VMEM((ROUNDS * EDGES, WIDE), F32),
            pltpu.VMEM((PACKED, 128), F32),
            pltpu.VMEM((1408, 1), F32),
        ]
        + [tiles(2 * ROUNDS, TILES)] * 6
        + [
            tiles(256),
            tiles(128),
            tiles(128),
            tiles(2, 4, 16),
            tiles(2, 16),
            tiles(2, 4, 4),
            tiles(8),
            tiles(8),
            tiles(256),
            pltpu.SemaphoreType.DMA((2 * ROUNDS, 3)),
            pltpu.SemaphoreType.DMA((2 * ROUNDS, 3)),
            pltpu.SemaphoreType.DMA((12,)),
            pltpu.SemaphoreType.DMA((12,)),
        ],
        compiler_params=pltpu.CompilerParams(
            collective_id=0, has_side_effects=True, vmem_limit_bytes=48 * 1024 * 1024
        ),
    )(
        round_masks,
        edge_src,
        edge_rel,
        edge_count,
        embeddings,
        entity_state.reshape(1, ROWS),
        relations,
        relation_state.reshape(1, NREL),
        edge_src,
        edge_rel,
        edge_dst,
        neg_rows.reshape(ROUNDS, NEG),
    )
    return (new_rows, new_state.reshape(ROWS), new_relations, new_relation_state.reshape(NREL))


def solution(mesh):
    placed = (
        P("dom", None),
        P("dom"),
        P(),
        P(),
        P(),
        P(None, "dom"),
        P(None, "dom"),
        P(None, "dom"),
        P(None, "dom"),
        P(None, "dom", None),
    )
    return jax.shard_map(
        shards,
        mesh=mesh,
        in_specs=placed,
        out_specs=(P("dom", None), P("dom"), P(), P()),
        check_vma=False,
    )
```

time: 623 us -> 147 us (0.24); the launches traced: 614 us -> 147 us
  waiting for transfers between devices: 423 us -> 0 us
  Pallas kernels: 0 us -> 133 us
  starting transfers between devices: 65.3 us -> 0 us
  other arithmetic: 55.3 us -> 0.62 us
  between operations: 25.5 us -> 0.72 us
  local copies, waits for them, and re-layouts: 35.5 us -> 12.1 us
  matrix products: 9.42 us -> 0 us
    psum x1 -> x0, waiting for transfers between devices: 245 us -> none  [shards(): rel_total = lax.psum(rel_total, 'dom')]
    ppermute x32 -> x0, waiting for transfers between devices: 179 us -> none  [from_partner(): return lax.ppermute(value, axis, pairs)]
    pallas_call x0 -> x1, Pallas kernels: none -> 133 us  [shards(): pl.pallas_call(kernel, out_shape=(jax.ShapeDtypeStruct((ROWS, D), F32), j...]
    ppermute x32 -> x0, starting transfers between devices: 65.2 us -> none  [from_partner(): return lax.ppermute(value, axis, pairs)]
    scatter-add x6 -> x0, other arithmetic: 23.2 us -> none  [the longest x2 15.1 us: bucket_grads(): dest_grads = dest_grads.at[neg_ids.reshape(-1)].add(row_terms)]
    gather x14 -> x0, local copies, waits for them, and re-layouts: 21 us -> none  [the longest x2 10.1 us: bucket_grads(): neg_table = table[neg_ids]]
    select_n x35 -> x0, other arithmetic: 12.6 us -> none  [the longest x16 8.05 us: rows_across(): payload = jnp.where(bit_is_set(round_mask, hop_index), moved, payload)]
    dot_general x6 -> x0, matrix products: 9.42 us -> none  [the longest x2 3.51 us: bucket_grads(): jnp.einsum('cen,ced->cnd', neg_coef, blocks, preferred_element_type=jnp.f...]
  transfers between devices with their start and end apart: 33 -> 0, of which waited for: 31 -> 0; matrix products, arithmetic and copies ran while one was open for 5% -> 0% of each run, Pallas kernels for 0% -> 0%
where the time goes in v1:
time: 147 us
  Pallas kernels  133 us (90%)
  local copies, waits for them, and re-layouts  12.1 us (8%)
    pallas_call x1, Pallas kernels, shards(): pl.pallas_call(kernel, out_shape=(jax.ShapeDtypeStruct((ROWS, D), F32), j...  133 us
    unnamed x19, local copies, waits for them, and re-layouts  11.4 us

profile of v1, /device:TPU:1, one launch (start us, length us, event | category | flops | bytes accessed | tf_op | source)
XLA Modules:
  0.0 146.6 jit_solution(579446790890929914)
XLA Ops:
  0.6 0.7 copy.14.counts
  1.4 0.7 reshape.24.rel_state_in
  2.1 0.7 copy.21
  2.8 1.2 copy.15.emb_in
  4.0 0.0 copy-start.1
  4.0 0.0 copy-start.2
  4.0 0.0 copy-start.3
  4.0 0.0 copy-start.4
  4.0 0.0 copy-start.5
  4.0 3.4 %copy.16.relations = f32[1300,400]{1,0:T(8,128)} copy(f32[1300,400]{0,1:T(8,128)} %param.12) | data formatting | bytes 4160000 | tf_op args[2]
  7.4 0.0 copy-done.1
  7.4 0.0 copy-done.2
  7.4 0.0 copy-done.3
  7.4 0.0 copy-done.4
  7.5 0.0 copy-done.5
  7.5 133.1 %shard_map.129 = (f32[256,400]{1,0:T(8,128)S(1)}, f32[1,256]{1,0:T(1,128)S(1)}, f32[1300,400]{1,0:T(8,128)S(1)}, f32[1,1300]{1,0:T(1,128)S(1)}) custom-call(s32[2]{0:T(128)S(1)} %copy-done.5, s32[2,128]{1,0:T(2,128)S(1)} %copy-done.1, s32[2,128]{1,0:T(2,128)S(1)} %copy-done.2, s32[2,1]{1,0:T(2,128)S(1)} %copy.14.counts, f32[256,400]{1,0:T(8,128)S(1)} %copy.15.emb_in, ...), custom_call_target="tpu_custom_call" | custom-call | tf_op jit(solution)/shard_map/pallas_call | solution.py:470
  140.6 0.0 copy-start
  140.6 0.8 copy-done
  141.4 2.0 %copy.17 = f32[256,400]{0,1:T(8,128)} copy(f32[256,400]{1,0:T(8,128)} %copy-done) | data formatting | bytes 819200
  143.3 0.6 reduce
  144.0 2.1 %copy.18 = f32[1300,400]{0,1:T(8,128)} copy(f32[1300,400]{1,0:T(8,128)S(1)} %get-tuple-element.14) | data formatting | bytes 4160000
  146.0 0.6 copy.23
Async XLA Ops:
  4.0 3.5 %copy-start.1 = (s32[2,128]{1,0:T(2,128)S(1)}, s32[2,128]{1,0:T(2,128)}, u32[]{:S(2)}) copy-start(s32[2,128]{1,0:T(2,128)} %src_rows.1) | copy-start | bytes 3076
  4.0 3.4 %copy-start.2 = (s32[2,128]{1,0:T(2,128)S(1)}, s32[2,128]{1,0:T(2,128)}, u32[]{:S(2)}) copy-start(s32[2,128]{1,0:T(2,128)} %rel_rows.1) | copy-start | bytes 3076
  4.0 3.4 %copy-start.3 = (f32[256]{0:T(256)S(1)}, f32[256]{0:T(256)}, u32[]{:S(2)}) copy-start(f32[256]{0:T(256)} %param.11) | copy-start | bytes 3076
  4.0 3.4 %copy-start.4 = (s32[2,128]{1,0:T(2,128)S(1)}, s32[2,128]{1,0:T(2,128)}, u32[]{:S(2)}) copy-start(s32[2,128]{1,0:T(2,128)} %dst_rows.1) | copy-start | bytes 3076
  4.0 3.4 %copy-start.5 = (s32[2]{0:T(128)S(1)}, s32[2]{0:T(128)}, u32[]{:S(2)}) copy-start(s32[2]{0:T(128)} %masks.1) | copy-start | bytes 28
  140.6 0.8 copy-start

commit v2 on v1

v2 whole, which is shorter than its diff:
```python
import jax
import jax.numpy as jnp
from jax import lax
from jax.experimental import pallas as pl
from jax.experimental.pallas import tpu as pltpu
from jax.sharding import PartitionSpec as P

ROUNDS = 2
D = 400
NREL = 1300
NEG = 1000
ROWS = 256
EDGES = 128
WIDE = 512
LEFT = D - 384
DEVICES = 256
TILES = 76
REL_PAD = 1408
BLOCK = 1304
GROUP = 168
PACKED = 4096

learning_rate = 0.1

F32 = jnp.float32
BF16 = jnp.bfloat16


def iota(shape, dim):
    return lax.broadcasted_iota(jnp.int32, shape, dim)


def dot(a, b, left=1, right=0):
    return lax.dot_general(a, b, (((left,), (right,)), ((), ())), preferred_element_type=F32)


def halves(value):
    high = value.astype(BF16)
    return high, (value - high.astype(F32)).astype(BF16)


def as_column(row):
    count = row.shape[1]
    square = (count, count)
    return jnp.sum(jnp.where(iota(square, 0) == iota(square, 1), row, 0.0), axis=1, keepdims=True)


def as_row(column):
    count = column.shape[0]
    square = (count, count)
    return jnp.sum(jnp.where(iota(square, 0) == iota(square, 1), column, 0.0), axis=0, keepdims=True)


def remote(source, target, send, recv, device):
    return pltpu.make_async_remote_copy(
        src_ref=source,
        dst_ref=target,
        send_sem=send,
        recv_sem=recv,
        device_id=(device,),
        device_id_type=pl.DeviceIdType.MESH,
    )


def await_bytes(ref, sem):
    pltpu.make_async_copy(ref, ref, sem).wait()


def carrier(tile):
    return (10 * tile) // 3


def kernel(
    masks_hbm,
    src_hbm,
    rel_hbm,
    counts_hbm,
    emb_hbm,
    state_hbm,
    relations_hbm,
    rel_state_hbm,
    dst_hbm,
    neg_hbm,
    emb_out,
    state_out,
    rel_out,
    rel_state_out,
    masks,
    src_ids,
    rel_ids,
    counts,
    emb_in,
    state_in,
    rel_in,
    rel_state_in,
    src_rows,
    rel_rows,
    dst_rows,
    neg_rows,
    emb,
    relations,
    srcs,
    rels,
    table,
    vec,
    far_table,
    far_vec,
    grads,
    is_rel,
    packed,
    state_col,
    x1,
    held_0,
    held_1,
    x2,
    arrived,
    t0,
    r0,
    t1,
    ra,
    t2,
    rb,
    t3,
    rz,
    gathered,
    send,
    recv,
    sum_send,
    sum_recv,
    loaded,
):
    loads = [
        pltpu.make_async_copy(source, target, loaded.at[n])
        for n, (source, target) in enumerate(
            (
                (emb_hbm, emb_in),
                (relations_hbm, rel_in),
                (src_hbm, src_ids),
                (rel_hbm, rel_ids),
                (masks_hbm, masks),
                (counts_hbm, counts),
                (state_hbm, state_in),
                (rel_state_hbm, rel_state_in),
                (src_hbm, src_rows),
                (rel_hbm, rel_rows),
                (dst_hbm, dst_rows),
                (neg_hbm, neg_rows),
            )
        )
    ]
    for load in loads:
        load.start()
    me = lax.axis_index("dom")
    c = me % 2
    y = (me // 2) % 4
    x = (me // 8) % 4
    z = me // 32
    mine = (3 * me + 2) // 10
    active = jnp.logical_and(carrier(mine) == me, mine < TILES)
    idle = jnp.logical_not(active)
    first_tile = (me * TILES) // DEVICES

    def at_x(to):
        return ((z * 4 + to) * 4 + y) * 2 + c

    def at_y(to):
        return ((z * 4 + x) * 4 + to) * 2 + c

    def at_z(to):
        return ((to * 4 + x) * 4 + y) * 2 + c

    other = me + 1 - 2 * c

    barrier = pltpu.get_barrier_semaphore()

    def tell(device):
        pl.semaphore_signal(barrier, inc=1, device_id=(device,), device_id_type=pl.DeviceIdType.MESH)

    def tell_all(step, _):
        tell((me + step) % DEVICES)
        return 0

    def tell_carriers(step, _):
        tell(carrier((first_tile + step) % TILES))
        return 0

    @pl.when(active)
    def _():
        lax.fori_loop(1, DEVICES, tell_all, 0)

    @pl.when(idle)
    def _():
        lax.fori_loop(0, TILES, tell_carriers, 0)

    for step in range(1, 4):
        tell(at_x((x + step) % 4))
        tell(at_y((y + step) % 4))
    for step in range(1, 8):
        tell(at_z((z + step) % 8))
    tell(other)

    def gather_rels(r):
        for e in range(EDGES):
            rels[r, e : e + 1, :] = relations[pl.ds(rel_ids[r, e], 1), :]

    def gather_srcs(r):
        for e in range(EDGES):
            srcs[r, e : e + 1, :] = emb[pl.ds(src_ids[r, e], 1), :]

    def hit_row(r):
        hits = jnp.sum((iota((ROWS, NEG), 0) == neg_rows[r]).astype(F32), axis=1, keepdims=True)
        return jnp.concatenate([as_row(hits[:128]), as_row(hits[128:])], axis=1)

    def bucket_rows(r):
        dst = dst_rows[r : r + 1, :].astype(F32)
        live = (iota((1, EDGES), 1) < counts[r]).astype(F32)
        return dst, live, hit_row(r)

    def pack(r, first, rows):
        for i in range(8):
            for j in range(3):
                x1[r, first + 3 * i + j] = rows[16 * i : 16 * i + 16, 128 * j : 128 * j + 128]
        last = rows[:, 384:].astype(F32)
        tail = last[:16]
        for g in range(1, 8):
            tail = tail + pltpu.roll(last[16 * g : 16 * g + 16], LEFT * g, 1)
        x1[r, first + 24] = tail.astype(BF16)

    def unpack(r, first, target, at):
        for i in range(8):
            for j in range(3):
                target[at + 16 * i : at + 16 * i + 16, 128 * j : 128 * j + 128] = arrived[r, first + 3 * i + j]
        tail = arrived[r, first + 24].astype(F32)
        inside = iota((16, 128), 1) < LEFT
        for g in range(8):
            part = pltpu.roll(tail, 128 - LEFT * g, 1) if g else tail
            target[at + 16 * g : at + 16 * g + 16, 384:] = jnp.where(inside, part, 0.0).astype(BF16)

    def pack_table(r):
        table[...] = emb[...].astype(BF16)
        pack(r, 0, table[0:128, :])
        pack(r, 25, table[128:256, :])

    def pack_vectors(r, rows):
        dst, live, hits = rows
        vec[...] = (srcs[r] * rels[r]).astype(BF16)
        pack(r, 50, vec[...])
        high = jnp.floor(hits * (1.0 / 16.0))
        low = hits - 16.0 * high
        extras = (dst, live, high[:, :128], high[:, 128:], low[:, :128], low[:, 128:])
        sub = iota((16, 128), 0)
        meta = jnp.zeros((16, 128), F32)
        for n, extra in enumerate(extras):
            meta = jnp.where(sub == n, extra, meta)
        x1[r, 75] = meta.astype(BF16)

    def exchange(r, mask, during):
        held = (held_0, held_1)[r]

        def outward(step, _):
            i = (first_tile + step) % TILES
            device = carrier(i)

            @pl.when(device != me)
            def _():
                remote(x1.at[r, i], held.at[me], send.at[r, 0], recv.at[r, 0], device).start()

            @pl.when(device == me)
            def _():
                held[me] = x1[r, i]

            return 0

        lax.fori_loop(0, TILES, outward, 0)
        during()

        @pl.when(active)
        def _():
            await_bytes(held.at[pl.ds(0, DEVICES - 1)], recv.at[r, 0])

            def onward(step, _):
                base = 16 * ((me // 16 + step) % 16)
                for n in range(16):
                    x2[r, base + n] = held[lax.bitwise_xor(mask, base + n)]
                for n in range(16):
                    device = base + n

                    @pl.when(device != me)
                    def _():
                        remote(x2.at[r, device], arrived.at[r, mine], send.at[r, 1], recv.at[r, 1], device).start()

                return 0

            lax.fori_loop(0, 16, onward, 0)
            arrived[r, mine] = x2[r, me]
            await_bytes(arrived.at[r, pl.ds(0, TILES - 1)], recv.at[r, 1])

        @pl.when(idle)
        def _():
            await_bytes(arrived.at[r], recv.at[r, 1])

        unpack(r, 0, far_table, 0)
        unpack(r, 25, far_table, 128)
        unpack(r, 50, far_vec, 0)

    def sent(r):
        @pl.when(active)
        def _():
            await_bytes(x1.at[r, pl.ds(0, TILES - 1)], send.at[r, 0])
            await_bytes(x2.at[r, pl.ds(0, DEVICES - 1)], send.at[r, 1])

        @pl.when(idle)
        def _():
            await_bytes(x1.at[r], send.at[r, 0])

    def coefficients(vectors, rows, ends):
        dst, live, hits = ends
        scores = dot(vectors, rows, 1, 1)
        dst = as_column(dst)
        live = as_column(live)
        is_dst = iota((EDGES, ROWS), 1).astype(F32) == dst
        neg_coef = (live * (1.0 / (1.0 + jnp.exp(-scores))) / NEG).astype(BF16).astype(F32)
        positive = jnp.sum(jnp.where(is_dst, scores, 0.0), axis=1, keepdims=True)
        pos_coef = -live * (1.0 / (1.0 + jnp.exp(positive)))
        return halves(neg_coef * hits + jnp.where(is_dst, pos_coef, 0.0))

    for load in loads:
        load.wait()
    emb[:, 384:] = jnp.zeros((ROWS, 128), F32)
    for j in range(4):
        depth = min(128, D - 128 * j)
        for i in range(2):
            emb[128 * i : 128 * i + 128, 128 * j : 128 * j + depth] = emb_in[
                128 * j : 128 * j + depth, 128 * i : 128 * i + 128
            ].T
    pack_table(0)
    relations[:, 384:] = jnp.zeros((REL_PAD, 128), F32)
    for j in range(4):
        depth = min(128, D - 128 * j)
        for i in range(11):
            width = min(128, NREL - 128 * i)
            part = rel_in[128 * j : 128 * j + depth, 128 * i : 128 * i + width]
            if width < 128:
                part = jnp.concatenate([part, jnp.ones((depth, 128 - width), F32)], axis=1)
            relations[128 * i : 128 * i + 128, 128 * j : 128 * j + depth] = part.T
    gather_rels(0)
    gather_srcs(0)
    near = bucket_rows(0)
    pack_vectors(0, near)
    state = jnp.concatenate([as_column(state_in[:, :128]), as_column(state_in[:, 128:])], axis=0)

    @pl.when(active)
    def _():
        pl.semaphore_wait(barrier, DEVICES - 1 + 14)

    @pl.when(idle)
    def _():
        pl.semaphore_wait(barrier, TILES + 14)

    def prepare():
        gather_rels(1)
        later.append(bucket_rows(1))
        for n in range(11):
            width = min(128, NREL - 128 * n)
            part = rel_state_in[128 * n : 128 * n + width].reshape(1, width)
            if width < 128:
                part = jnp.concatenate([part, jnp.ones((1, 128 - width), F32)], axis=1)
            state_col[128 * n : 128 * n + 128, :] = as_column(part)

    def prepare_sum():
        ids = jnp.concatenate([rel_rows[0:1, :], rel_rows[1:2, :]], axis=1)
        for g in range(8):
            at = GROUP * g
            is_rel[at : at + GROUP, :] = (iota((GROUP, ROUNDS * EDGES), 0) + at == ids).astype(BF16)

    later = []
    for r in range(ROUNDS):
        exchange(r, masks[r], prepare if r == 0 else prepare_sum)
        meta = arrived[r, 75].astype(F32)
        hits = jnp.concatenate([16.0 * meta[n : n + 1] + meta[n + 2 : n + 3] for n in (2, 3)], axis=1)
        far = (meta[0:1], meta[1:2], hits)

        high, low = coefficients(vec[...], far_table[...], near)
        pulled = (dot(high, far_table[...]) + dot(low, far_table[...])).astype(BF16).astype(F32)
        high, low = coefficients(far_vec[...], table[...], far)
        pushed = (dot(high, far_vec[...], 0, 0) + dot(low, far_vec[...], 0, 0)).astype(BF16).astype(F32)

        grads[r * EDGES : (r + 1) * EDGES, :] = (pulled * srcs[r]).astype(BF16)
        is_src = (iota((ROWS, EDGES), 0) == src_rows[r : r + 1, :]).astype(BF16)
        high, low = halves(pulled * rels[r])
        grad = pushed + dot(is_src, high) + dot(is_src, low)
        state = state + jnp.sum(grad * grad, axis=1, keepdims=True) * (1.0 / D)
        emb[...] = emb[...] - learning_rate * grad / jnp.sqrt(state)
        if r + 1 < ROUNDS:
            pack_table(r + 1)
            gather_srcs(r + 1)
            near = later[r]
            pack_vectors(r + 1, near)

    tail = jnp.zeros((GROUP, 128), F32)
    for g in range(8):
        rows = min(GROUP, BLOCK - GROUP * g)
        part = dot(is_rel[GROUP * g : GROUP * g + GROUP, :], grads[...])
        for n in range(3):
            at = BLOCK * n + GROUP * g
            packed[at : at + rows, :] = part[:rows, 128 * n : 128 * n + 128]
        end = part[:, 384:]
        tail = tail + (pltpu.roll(end, LEFT * g, 1) if g else end)
    packed[3 * BLOCK : 3 * BLOCK + GROUP, :] = tail
    packed[3 * BLOCK + GROUP :, :] = jnp.zeros((PACKED - 3 * BLOCK - GROUP, 128), F32)
    t0[...] = packed[...].reshape(256, 16, 128).astype(BF16)

    remote(t0.at[pl.ds((1 - c) * 128, 128)], r0, sum_send.at[0], sum_recv.at[0], other).start()
    await_bytes(r0, sum_recv.at[0])
    t1[...] = (t0[pl.ds(c * 128, 128)].astype(F32) + r0[...].astype(F32)).astype(BF16)

    for step in range(1, 4):
        to_x, to_y = (x + step) % 4, (y + step) % 4
        remote(t1.at[pl.ds(16 * to_x, 16)], ra.at[0, x], sum_send.at[1], sum_recv.at[1], at_x(to_x)).start()
        remote(t1.at[pl.ds(64 + 16 * to_y, 16)], ra.at[1, y], sum_send.at[2], sum_recv.at[2], at_y(to_y)).start()
    ra[0, x] = t1[pl.ds(16 * x, 16)]
    ra[1, y] = t1[pl.ds(64 + 16 * y, 16)]

    def added(ref, lead, count):
        total = ref[lead + (0,)].astype(F32)
        for n in range(1, count):
            total = total + ref[lead + (n,)].astype(F32)
        return total.astype(BF16)

    await_bytes(ra.at[0, pl.ds(0, 3)], sum_recv.at[1])
    t2[0] = added(ra, (0,), 4)
    for step in range(1, 4):
        to_y = (y + step) % 4
        remote(t2.at[0, pl.ds(4 * to_y, 4)], rb.at[0, y], sum_send.at[3], sum_recv.at[3], at_y(to_y)).start()
    rb[0, y] = t2[0, pl.ds(4 * y, 4)]
    await_bytes(ra.at[1, pl.ds(0, 3)], sum_recv.at[2])
    t2[1] = added(ra, (1,), 4)
    for step in range(1, 4):
        to_x = (x + step) % 4
        remote(t2.at[1, pl.ds(4 * to_x, 4)], rb.at[1, x], sum_send.at[4], sum_recv.at[4], at_x(to_x)).start()
    rb[1, x] = t2[1, pl.ds(4 * x, 4)]
    await_bytes(rb.at[0, pl.ds(0, 3)], sum_recv.at[3])
    t3[0:4] = added(rb, (0,), 4)
    await_bytes(rb.at[1, pl.ds(0, 3)], sum_recv.at[4])
    t3[4:8] = added(rb, (1,), 4)

    def spread_z(step, _):
        to = (z + step) % 8
        remote(t3.at[to], rz.at[z], sum_send.at[5], sum_recv.at[5], at_z(to)).start()
        return 0

    lax.fori_loop(1, 8, spread_z, 0)
    rz[z] = t3[z]
    await_bytes(rz.at[pl.ds(0, 7)], sum_recv.at[5])

    which = z // 4
    base_x = c * 128 + 16 * x + 4 * y
    base_y = c * 128 + 64 + 16 * y + 4 * x
    spot = (1 - which) * base_x + which * base_y + z % 4
    gathered[spot] = added(rz, (), 8)

    def gather_z(step, _):
        to = (z + step) % 8
        remote(gathered.at[spot], gathered.at[spot], sum_send.at[6], sum_recv.at[6], at_z(to)).start()
        return 0

    lax.fori_loop(1, 8, gather_z, 0)
    await_bytes(gathered.at[pl.ds(0, 7)], sum_recv.at[6])

    def whole(first, count, n, device):
        part = gathered.at[pl.ds(first, count)]
        return remote(part, part, sum_send.at[n], sum_recv.at[n], device)

    for step in range(1, 4):
        to_x, to_y = (x + step) % 4, (y + step) % 4
        whole(base_x, 4, 7, at_y(to_y)).start()
        whole(base_y, 4, 8, at_x(to_x)).start()
    await_bytes(gathered.at[pl.ds(0, 12)], sum_recv.at[7])
    await_bytes(gathered.at[pl.ds(0, 12)], sum_recv.at[8])
    for step in range(1, 4):
        to_x, to_y = (x + step) % 4, (y + step) % 4
        whole(c * 128 + 16 * x, 16, 9, at_x(to_x)).start()
        whole(c * 128 + 64 + 16 * y, 16, 10, at_y(to_y)).start()
    await_bytes(gathered.at[pl.ds(0, 48)], sum_recv.at[9])
    await_bytes(gathered.at[pl.ds(0, 48)], sum_recv.at[10])
    whole(c * 128, 128, 11, other).start()
    emb_out[...] = emb[:, :D]
    state_out[...] = jnp.concatenate([as_row(state[:128]), as_row(state[128:])], axis=1)
    await_bytes(gathered.at[pl.ds(0, 128)], sum_recv.at[11])

    packed[...] = gathered[...].astype(F32).reshape(PACKED, 128)
    for g in range(8):
        rows = min(GROUP, NREL - GROUP * g)
        at = GROUP * g
        parts = [packed[BLOCK * n + at : BLOCK * n + at + rows, :] for n in range(3)]
        end = packed[3 * BLOCK : 3 * BLOCK + GROUP, :]
        end = (pltpu.roll(end, 128 - LEFT * g, 1) if g else end)[:rows, :LEFT]
        squares = parts[0] * parts[0] + parts[1] * parts[1] + parts[2] * parts[2]
        mean = jnp.sum(squares, axis=1, keepdims=True) + jnp.sum(end * end, axis=1, keepdims=True)
        fresh = state_col[at : at + rows, :] + mean * (1.0 / D)
        state_col[at : at + rows, :] = fresh
        root = jnp.sqrt(fresh)
        for n in range(3):
            cols = slice(128 * n, 128 * n + 128)
            rel_out[at : at + rows, cols] = relations[at : at + rows, cols] - learning_rate * parts[n] / root
        rel_out[at : at + rows, 384:] = relations[at : at + rows, 384:D] - learning_rate * end / root
    for n in range(11):
        width = min(128, NREL - 128 * n)
        row = as_row(state_col[128 * n : 128 * n + 128, :])
        rel_state_out[:, 128 * n : 128 * n + width] = row[:, :width]

    for r in range(ROUNDS):
        sent(r)
    await_bytes(t0.at[pl.ds(0, 128)], sum_send.at[0])
    for n, tiles in ((1, 48), (2, 48), (3, 12), (4, 12), (5, 7), (6, 7), (7, 12), (8, 12), (9, 48), (10, 48), (11, 128)):
        await_bytes(gathered.at[pl.ds(0, tiles)], sum_send.at[n])


def shards(
    embeddings,
    entity_state,
    relations,
    relation_state,
    round_masks,
    edge_src,
    edge_rel,
    edge_dst,
    edge_count,
    neg_rows,
):
    vmem = pl.BlockSpec(memory_space=pltpu.VMEM)

    def tiles(*lead):
        return pltpu.VMEM(lead + (16, 128), BF16)

    new_rows, new_state, new_relations, new_relation_state = pl.pallas_call(
        kernel,
        out_shape=(
            jax.ShapeDtypeStruct((ROWS, D), F32),
            jax.ShapeDtypeStruct((1, ROWS), F32),
            jax.ShapeDtypeStruct((NREL, D), F32),
            jax.ShapeDtypeStruct((1, NREL), F32),
        ),
        in_specs=[pl.BlockSpec(memory_space=pltpu.HBM)] * 10,
        out_specs=(vmem,) * 4,
        scratch_shapes=[
            pltpu.SMEM((ROUNDS,), jnp.int32),
            pltpu.SMEM((ROUNDS, EDGES), jnp.int32),
            pltpu.SMEM((ROUNDS, EDGES), jnp.int32),
            pltpu.SMEM((ROUNDS,), jnp.int32),
            pltpu.VMEM((D, ROWS), F32),
            pltpu.VMEM((1, ROWS), F32),
            pltpu.VMEM((D, NREL), F32),
            pltpu.VMEM((NREL,), F32),
            pltpu.VMEM((ROUNDS, EDGES), jnp.int32),
            pltpu.VMEM((ROUNDS, EDGES), jnp.int32),
            pltpu.VMEM((ROUNDS, EDGES), jnp.int32),
            pltpu.VMEM((ROUNDS, 1, NEG), jnp.int32),
            pltpu.VMEM((ROWS, WIDE), F32),
            pltpu.VMEM((REL_PAD, WIDE), F32),
            pltpu.VMEM((ROUNDS, EDGES, WIDE), F32),
            pltpu.VMEM((ROUNDS, EDGES, WIDE), F32),
            pltpu.VMEM((ROWS, WIDE), BF16),
            pltpu.VMEM((EDGES, WIDE), BF16),
            pltpu.VMEM((ROWS, WIDE), BF16),
            pltpu.VMEM((EDGES, WIDE), BF16),
            pltpu.VMEM((ROUNDS * EDGES, WIDE), BF16),
            pltpu.VMEM((8 * GROUP, ROUNDS * EDGES), BF16),
            pltpu.VMEM((PACKED, 128), F32),
            pltpu.VMEM((REL_PAD, 1), F32),
            tiles(ROUNDS, TILES),
            tiles(DEVICES),
            tiles(DEVICES),
            tiles(ROUNDS, DEVICES),
            tiles(ROUNDS, TILES),
            tiles(256),
            tiles(128),
            tiles(128),
            tiles(2, 4, 16),
            tiles(2, 16),
            tiles(2, 4, 4),
            tiles(8),
            tiles(8),
            tiles(256),
            pltpu.SemaphoreType.DMA((ROUNDS, 2)),
            pltpu.SemaphoreType.DMA((ROUNDS, 2)),
            pltpu.SemaphoreType.DMA((12,)),
            pltpu.SemaphoreType.DMA((12,)),
            pltpu.SemaphoreType.DMA((12,)),
        ],
        compiler_params=pltpu.CompilerParams(
            collective_id=0, has_side_effects=True, vmem_limit_bytes=60 * 1024 * 1024
        ),
    )(
        round_masks,
        edge_src,
        edge_rel,
        edge_count.reshape(ROUNDS),
        embeddings.T,
        entity_state.reshape(1, ROWS),
        relations.T,
        relation_state,
        edge_dst,
        neg_rows,
    )
    return (new_rows, new_state.reshape(ROWS), new_relations, new_relation_state.reshape(NREL))


def solution(mesh):
    placed = (
        P("dom", None),
        P("dom"),
        P(),
        P(),
        P(),
        P(None, "dom"),
        P(None, "dom"),
        P(None, "dom"),
        P(None, "dom"),
        P(None, "dom", None),
    )
    return jax.shard_map(
        shards,
        mesh=mesh,
        in_specs=placed,
        out_specs=(P("dom", None), P("dom"), P(), P()),
        check_vma=False,
    )
```

time: 147 us -> 116 us (0.79)
  Pallas kernels: 133 us -> 109 us
  local copies, waits for them, and re-layouts: 12.1 us -> 5.68 us
    pallas_call x1, Pallas kernels: 133 us -> 109 us  [shards(): pl.pallas_call(kernel, out_shape=(jax.ShapeDtypeStruct((ROWS, D), F32), j...]
    unnamed x19 -> x7, local copies, waits for them, and re-layouts: 11.4 us -> 5.68 us
where the time goes in v2:
time: 116 us
  Pallas kernels  109 us (94%)
  local copies, waits for them, and re-layouts  5.68 us (5%)
    pallas_call x1, Pallas kernels, shards(): pl.pallas_call(kernel, out_shape=(jax.ShapeDtypeStruct((ROWS, D), F32), j...  109 us
    unnamed x7, local copies, waits for them, and re-layouts  5.68 us

profile of v2, /device:TPU:1, one launch (start us, length us, event | category | flops | bytes accessed | tf_op | source)
XLA Modules:
  0.0 115.5 jit_solution(10146298199301947505)
XLA Ops:
  0.6 108.6 %shard_map.129 = (f32[256,400]{1,0:T(8,128)}, f32[1,256]{1,0:T(1,128)}, f32[1300,400]{1,0:T(8,128)}, f32[1,1300]{1,0:T(1,128)}) custom-call(s32[2]{0:T(128)} %masks_hbm.1, s32[2,128]{1,0:T(2,128)} %src_hbm.1, s32[2,128]{1,0:T(2,128)} %rel_hbm.1, s32[2]{0:T(128)} %bitcast.9, f32[400,256]{1,0:T(8,128)} %bitcast.6, f32[1,256]{1,0:T(1,128)} %bitcast.7, ...), custom_call_target="tpu_custom_call" | custom-call | tf_op jit(solution)/shard_map/pallas_call | solution.py:536
  109.2 2.0 %copy.14 = f32[256,400]{0,1:T(8,128)} copy(f32[256,400]{1,0:T(8,128)} %get-tuple-element.12) | data formatting | bytes 819200
  111.2 0.0 copy-start
  111.2 0.0 copy-start.1
  111.2 3.1 %copy.15 = f32[1300,400]{0,1:T(8,128)} copy(f32[1300,400]{1,0:T(8,128)} %get-tuple-element.14) | data formatting | bytes 4160000
  114.3 0.0 copy-done
  114.3 0.6 reduce
  114.9 0.0 copy-done.1
  114.9 0.6 copy.17
Async XLA Ops:
  111.2 3.1 %copy-start = (f32[1,1300]{1,0:T(1,128)S(1)}, f32[1,1300]{1,0:T(1,128)}, u32[]{:S(2)}) copy-start(f32[1,1300]{1,0:T(1,128)} %get-tuple-element.11) | copy-start | bytes 15604
  111.2 3.8 %copy-start.1 = (f32[1,256]{1,0:T(1,128)S(1)}, f32[1,256]{1,0:T(1,128)}, u32[]{:S(2)}) copy-start(f32[1,256]{1,0:T(1,128)} %get-tuple-element.9) | copy-start | bytes 3076

commit v3 on v2

--- a/solution.py
+++ b/solution.py
@@ -13,7 +13,7 @@
 EDGES = 128
 WIDE = 512
 LEFT = D - 384
-DEVICES = 256
+CHIPS = 128
 TILES = 76
 REL_PAD = 1408
 BLOCK = 1304
@@ -66,8 +66,18 @@
     pltpu.make_async_copy(ref, ref, sem).wait()
 
 
+def ring(offset):
+    return min(offset, 4 - offset)
+
+
+OFFSETS = sorted(
+    ((dx, dy) for dx in range(4) for dy in range(4)),
+    key=lambda offset: -ring(offset[0]) - ring(offset[1]),
+)
+
+
 def carrier(tile):
-    return (10 * tile) // 3
+    return (5 * tile) // 3
 
 
 def kernel(
@@ -113,13 +123,12 @@
     held_0,
     held_1,
     x2,
-    arrived,
+    arrived_0,
+    arrived_1,
     t0,
     r0,
     t1,
     ra,
-    t2,
-    rb,
     t3,
     rz,
     gathered,
@@ -127,6 +136,10 @@
     recv,
     sum_send,
     sum_recv,
+    core_send,
+    core_recv,
+    gather_send,
+    gather_recv,
     loaded,
 ):
     loads = [
@@ -155,19 +168,33 @@
     y = (me // 2) % 4
     x = (me // 8) % 4
     z = me // 32
-    mine = (3 * me + 2) // 10
-    active = jnp.logical_and(carrier(mine) == me, mine < TILES)
+    chip = me // 2
+    mine = (3 * chip + 2) // 5
+    active = jnp.logical_and(carrier(mine) == chip, mine < TILES)
     idle = jnp.logical_not(active)
-    first_tile = (me * TILES) // DEVICES
-
-    def at_x(to):
-        return ((z * 4 + to) * 4 + y) * 2 + c
-
-    def at_y(to):
-        return ((z * 4 + x) * 4 + to) * 2 + c
+
+    def plane(step):
+        return (z + 4 + ((step + 1) // 2) * (1 - 2 * (step % 2))) % 8
+
+    def first_tile(at):
+        return (48 * at + 4) // 5
+
+    def over_tiles(go):
+        def one_plane(step, _):
+            at = plane(step)
+            lax.fori_loop(first_tile(at), jnp.minimum(first_tile(at + 1), TILES), go, 0)
+            return 0
+
+        lax.fori_loop(0, 8, one_plane, 0)
+
+    places = [((x + dx) % 4) * 4 + (y + dy) % 4 for dx, dy in OFFSETS]
+    place = places[-1]
+
+    def at_place(to):
+        return (z * 16 + to) * 2 + c
 
     def at_z(to):
-        return ((to * 4 + x) * 4 + y) * 2 + c
+        return (to * 16 + place) * 2 + c
 
     other = me + 1 - 2 * c
 
@@ -177,26 +204,34 @@
         pl.semaphore_signal(barrier, inc=1, device_id=(device,), device_id_type=pl.DeviceIdType.MESH)
 
     def tell_all(step, _):
-        tell((me + step) % DEVICES)
+        def tell_chip(n, _):
+            to = 16 * plane(step) + n
+
+            @pl.when(to != chip)
+            def _():
+                tell(2 * to + c)
+
+            return 0
+
+        lax.fori_loop(0, 16, tell_chip, 0)
         return 0
 
-    def tell_carriers(step, _):
-        tell(carrier((first_tile + step) % TILES))
+    def tell_carrier(i, _):
+        tell(2 * carrier(i) + c)
         return 0
 
     @pl.when(active)
     def _():
-        lax.fori_loop(1, DEVICES, tell_all, 0)
+        lax.fori_loop(0, 8, tell_all, 0)
 
     @pl.when(idle)
     def _():
-        lax.fori_loop(0, TILES, tell_carriers, 0)
-
-    for step in range(1, 4):
-        tell(at_x((x + step) % 4))
-        tell(at_y((y + step) % 4))
-    for step in range(1, 8):
-        tell(at_z((z + step) % 8))
+        over_tiles(tell_carrier)
+
+    for to in places[:-1]:
+        tell(at_place(to))
+    for step in range(7):
+        tell(at_z(plane(step)))
     tell(other)
 
     def gather_rels(r):
@@ -226,11 +261,11 @@
             tail = tail + pltpu.roll(last[16 * g : 16 * g + 16], LEFT * g, 1)
         x1[r, first + 24] = tail.astype(BF16)
 
-    def unpack(r, first, target, at):
+    def unpack(arrived, side, first, target, at):
         for i in range(8):
             for j in range(3):
-                target[at + 16 * i : at + 16 * i + 16, 128 * j : 128 * j + 128] = arrived[r, first + 3 * i + j]
-        tail = arrived[r, first + 24].astype(F32)
+                target[at + 16 * i : at + 16 * i + 16, 128 * j : 128 * j + 128] = arrived[side, first + 3 * i + j]
+        tail = arrived[side, first + 24].astype(F32)
         inside = iota((16, 128), 1) < LEFT
         for g in range(8):
             part = pltpu.roll(tail, 128 - LEFT * g, 1) if g else tail
@@ -256,62 +291,70 @@
 
     def exchange(r, mask, during):
         held = (held_0, held_1)[r]
-
-        def outward(step, _):
-            i = (first_tile + step) % TILES
-            device = carrier(i)
-
-            @pl.when(device != me)
+        arrived = (arrived_0, arrived_1)[r]
+        chip_mask = lax.shift_right_logical(mask, 1)
+        side = lax.bitwise_and(mask, 1)
+
+        def outward(i, _):
+            to = carrier(i)
+
+            @pl.when(to != chip)
             def _():
-                remote(x1.at[r, i], held.at[me], send.at[r, 0], recv.at[r, 0], device).start()
-
-            @pl.when(device == me)
+                remote(x1.at[r, i], held.at[chip], send.at[r, 0], recv.at[r, 0], 2 * to + c).start()
+
+            @pl.when(to == chip)
             def _():
-                held[me] = x1[r, i]
+                held[chip] = x1[r, i]
 
             return 0
 
-        lax.fori_loop(0, TILES, outward, 0)
+        over_tiles(outward)
         during()
 
         @pl.when(active)
         def _():
-            await_bytes(held.at[pl.ds(0, DEVICES - 1)], recv.at[r, 0])
+            await_bytes(held.at[pl.ds(0, CHIPS - 1)], recv.at[r, 0])
 
             def onward(step, _):
-                base = 16 * ((me // 16 + step) % 16)
+                base = 16 * plane(step)
                 for n in range(16):
-                    x2[r, base + n] = held[lax.bitwise_xor(mask, base + n)]
-                for n in range(16):
-                    device = base + n
-
-                    @pl.when(device != me)
+                    x2[r, base + n] = held[lax.bitwise_xor(chip_mask, base + n)]
+                for n in places:
+                    to = base + n
+
+                    @pl.when(to != chip)
                     def _():
-                        remote(x2.at[r, device], arrived.at[r, mine], send.at[r, 1], recv.at[r, 1], device).start()
+                        remote(x2.at[r, to], arrived.at[0, mine], send.at[r, 1], recv.at[r, 1], 2 * to + c).start()
 
                 return 0
 
-            lax.fori_loop(0, 16, onward, 0)
-            arrived[r, mine] = x2[r, me]
-            await_bytes(arrived.at[r, pl.ds(0, TILES - 1)], recv.at[r, 1])
+            lax.fori_loop(0, 8, onward, 0)
+            arrived[0, mine] = x2[r, chip]
+            await_bytes(arrived.at[0, pl.ds(0, TILES - 1)], recv.at[r, 1])
 
         @pl.when(idle)
         def _():
-            await_bytes(arrived.at[r], recv.at[r, 1])
-
-        unpack(r, 0, far_table, 0)
-        unpack(r, 25, far_table, 128)
-        unpack(r, 50, far_vec, 0)
+            await_bytes(arrived.at[0], recv.at[r, 1])
+
+        remote(arrived.at[0], arrived.at[1], send.at[r, 2], recv.at[r, 2], other).start()
+        await_bytes(arrived.at[1], recv.at[r, 2])
+
+        unpack(arrived, side, 0, far_table, 0)
+        unpack(arrived, side, 25, far_table, 128)
+        unpack(arrived, side, 50, far_vec, 0)
+        return arrived[side, 75].astype(F32)
 
     def sent(r):
         @pl.when(active)
         def _():
             await_bytes(x1.at[r, pl.ds(0, TILES - 1)], send.at[r, 0])
-            await_bytes(x2.at[r, pl.ds(0, DEVICES - 1)], send.at[r, 1])
+            await_bytes(x2.at[r, pl.ds(0, CHIPS - 1)], send.at[r, 1])
 
         @pl.when(idle)
         def _():
             await_bytes(x1.at[r], send.at[r, 0])
+
+        await_bytes(x1.at[r], send.at[r, 2])
 
     def coefficients(vectors, rows, ends):
         dst, live, hits = ends
@@ -351,11 +394,11 @@
 
     @pl.when(active)
     def _():
-        pl.semaphore_wait(barrier, DEVICES - 1 + 14)
+        pl.semaphore_wait(barrier, CHIPS - 1 + 23)
 
     @pl.when(idle)
     def _():
-        pl.semaphore_wait(barrier, TILES + 14)
+        pl.semaphore_wait(barrier, TILES + 23)
 
     def prepare():
         gather_rels(1)
@@ -375,8 +418,7 @@
 
     later = []
     for r in range(ROUNDS):
-        exchange(r, masks[r], prepare if r == 0 else prepare_sum)
-        meta = arrived[r, 75].astype(F32)
+        meta = exchange(r, masks[r], prepare if r == 0 else prepare_sum)
         hits = jnp.concatenate([16.0 * meta[n : n + 1] + meta[n + 2 : n + 3] for n in (2, 3)], axis=1)
         far = (meta[0:1], meta[1:2], hits)
 
@@ -410,83 +452,52 @@
     packed[3 * BLOCK + GROUP :, :] = jnp.zeros((PACKED - 3 * BLOCK - GROUP, 128), F32)
     t0[...] = packed[...].reshape(256, 16, 128).astype(BF16)
 
-    remote(t0.at[pl.ds((1 - c) * 128, 128)], r0, sum_send.at[0], sum_recv.at[0], other).start()
-    await_bytes(r0, sum_recv.at[0])
-    t1[...] = (t0[pl.ds(c * 128, 128)].astype(F32) + r0[...].astype(F32)).astype(BF16)
-
-    for step in range(1, 4):
-        to_x, to_y = (x + step) % 4, (y + step) % 4
-        remote(t1.at[pl.ds(16 * to_x, 16)], ra.at[0, x], sum_send.at[1], sum_recv.at[1], at_x(to_x)).start()
-        remote(t1.at[pl.ds(64 + 16 * to_y, 16)], ra.at[1, y], sum_send.at[2], sum_recv.at[2], at_y(to_y)).start()
-    ra[0, x] = t1[pl.ds(16 * x, 16)]
-    ra[1, y] = t1[pl.ds(64 + 16 * y, 16)]
-
-    def added(ref, lead, count):
-        total = ref[lead + (0,)].astype(F32)
+    for k, to in enumerate(places):
+        piece = pl.ds((1 - c) * 128 + 8 * to, 8)
+        remote(t0.at[piece], r0.at[pl.ds(8 * to, 8)], core_send.at[k], core_recv.at[k], other).start()
+    for k, to in enumerate(places):
+        piece = pl.ds(8 * to, 8)
+        await_bytes(r0.at[piece], core_recv.at[k])
+        t1[piece] = (t0[pl.ds(c * 128 + 8 * to, 8)].astype(F32) + r0[piece].astype(F32)).astype(BF16)
+        if k < 15:
+            remote(t1.at[piece], ra.at[place], sum_send.at[0], sum_recv.at[0], at_place(to)).start()
+    ra[place] = t1[pl.ds(8 * place, 8)]
+    await_bytes(ra.at[pl.ds(0, 15)], sum_recv.at[0])
+
+    def added(ref, count):
+        total = ref[0].astype(F32)
         for n in range(1, count):
-            total = total + ref[lead + (n,)].astype(F32)
+            total = total + ref[n].astype(F32)
         return total.astype(BF16)
 
-    await_bytes(ra.at[0, pl.ds(0, 3)], sum_recv.at[1])
-    t2[0] = added(ra, (0,), 4)
-    for step in range(1, 4):
-        to_y = (y + step) % 4
-        remote(t2.at[0, pl.ds(4 * to_y, 4)], rb.at[0, y], sum_send.at[3], sum_recv.at[3], at_y(to_y)).start()
-    rb[0, y] = t2[0, pl.ds(4 * y, 4)]
-    await_bytes(ra.at[1, pl.ds(0, 3)], sum_recv.at[2])
-    t2[1] = added(ra, (1,), 4)
-    for step in range(1, 4):
-        to_x = (x + step) % 4
-        remote(t2.at[1, pl.ds(4 * to_x, 4)], rb.at[1, x], sum_send.at[4], sum_recv.at[4], at_x(to_x)).start()
-    rb[1, x] = t2[1, pl.ds(4 * x, 4)]
-    await_bytes(rb.at[0, pl.ds(0, 3)], sum_recv.at[3])
-    t3[0:4] = added(rb, (0,), 4)
-    await_bytes(rb.at[1, pl.ds(0, 3)], sum_recv.at[4])
-    t3[4:8] = added(rb, (1,), 4)
-
-    def spread_z(step, _):
-        to = (z + step) % 8
-        remote(t3.at[to], rz.at[z], sum_send.at[5], sum_recv.at[5], at_z(to)).start()
-        return 0
-
-    lax.fori_loop(1, 8, spread_z, 0)
+    t3[...] = added(ra, 16)
+    for step in range(7):
+        to = plane(step)
+        remote(t3.at[to], rz.at[z], sum_send.at[1], sum_recv.at[1], at_z(to)).start()
     rz[z] = t3[z]
-    await_bytes(rz.at[pl.ds(0, 7)], sum_recv.at[5])
-
-    which = z // 4
-    base_x = c * 128 + 16 * x + 4 * y
-    base_y = c * 128 + 64 + 16 * y + 4 * x
-    spot = (1 - which) * base_x + which * base_y + z % 4
-    gathered[spot] = added(rz, (), 8)
-
-    def gather_z(step, _):
-        to = (z + step) % 8
-        remote(gathered.at[spot], gathered.at[spot], sum_send.at[6], sum_recv.at[6], at_z(to)).start()
-        return 0
-
-    lax.fori_loop(1, 8, gather_z, 0)
-    await_bytes(gathered.at[pl.ds(0, 7)], sum_recv.at[6])
-
-    def whole(first, count, n, device):
-        part = gathered.at[pl.ds(first, count)]
-        return remote(part, part, sum_send.at[n], sum_recv.at[n], device)
-
-    for step in range(1, 4):
-        to_x, to_y = (x + step) % 4, (y + step) % 4
-        whole(base_x, 4, 7, at_y(to_y)).start()
-        whole(base_y, 4, 8, at_x(to_x)).start()
-    await_bytes(gathered.at[pl.ds(0, 12)], sum_recv.at[7])
-    await_bytes(gathered.at[pl.ds(0, 12)], sum_recv.at[8])
-    for step in range(1, 4):
-        to_x, to_y = (x + step) % 4, (y + step) % 4
-        whole(c * 128 + 16 * x, 16, 9, at_x(to_x)).start()
-        whole(c * 128 + 64 + 16 * y, 16, 10, at_y(to_y)).start()
-    await_bytes(gathered.at[pl.ds(0, 48)], sum_recv.at[9])
-    await_bytes(gathered.at[pl.ds(0, 48)], sum_recv.at[10])
-    whole(c * 128, 128, 11, other).start()
+    await_bytes(rz.at[pl.ds(0, 7)], sum_recv.at[1])
+
+    base = c * 128 + 8 * place
+    spot = base + z
+    gathered[spot] = added(rz, 8)
+    for step in range(7):
+        to = plane(step)
+        remote(gathered.at[spot], gathered.at[spot], sum_send.at[2], sum_recv.at[2], at_z(to)).start()
+    await_bytes(gathered.at[pl.ds(0, 7)], sum_recv.at[2])
+
+    own = gathered.at[pl.ds(base, 8)]
+    for k, to in enumerate(places[:-1]):
+        dx, dy = OFFSETS[k]
+        back = OFFSETS.index((-dx % 4, -dy % 4))
+        remote(own, own, gather_send.at[k], gather_recv.at[back], at_place(to)).start()
+    for k, to in [(15, place)] + list(enumerate(places[:-1])):
+        piece = gathered.at[pl.ds(c * 128 + 8 * to, 8)]
+        if k < 15:
+            await_bytes(piece, gather_recv.at[k])
+        remote(piece, piece, sum_send.at[3], sum_recv.at[3], other).start()
     emb_out[...] = emb[:, :D]
     state_out[...] = jnp.concatenate([as_row(state[:128]), as_row(state[128:])], axis=1)
-    await_bytes(gathered.at[pl.ds(0, 128)], sum_recv.at[11])
+    await_bytes(gathered.at[pl.ds(0, 128)], sum_recv.at[3])
 
     packed[...] = gathered[...].astype(F32).reshape(PACKED, 128)
     for g in range(8):
@@ -511,9 +522,12 @@
 
     for r in range(ROUNDS):
         sent(r)
-    await_bytes(t0.at[pl.ds(0, 128)], sum_send.at[0])
-    for n, tiles in ((1, 48), (2, 48), (3, 12), (4, 12), (5, 7), (6, 7), (7, 12), (8, 12), (9, 48), (10, 48), (11, 128)):
+    for k in range(16):
+        await_bytes(r0.at[pl.ds(0, 8)], core_send.at[k])
+    for n, tiles in ((0, 120), (1, 7), (2, 7), (3, 128)):
         await_bytes(gathered.at[pl.ds(0, tiles)], sum_send.at[n])
+    for k in range(15):
+        await_bytes(gathered.at[pl.ds(0, 8)], gather_send.at[k])
 
 
 def shards(
@@ -569,23 +583,26 @@
             pltpu.VMEM((PACKED, 128), F32),
             pltpu.VMEM((REL_PAD, 1), F32),
             tiles(ROUNDS, TILES),
-            tiles(DEVICES),
-            tiles(DEVICES),
-            tiles(ROUNDS, DEVICES),
-            tiles(ROUNDS, TILES),
+            tiles(CHIPS),
+            tiles(CHIPS),
+            tiles(ROUNDS, CHIPS),
+            tiles(2, TILES),
+            tiles(2, TILES),
             tiles(256),
             tiles(128),
             tiles(128),
-            tiles(2, 4, 16),
-            tiles(2, 16),
-            tiles(2, 4, 4),
+            tiles(16, 8),
             tiles(8),
             tiles(8),
             tiles(256),
-            pltpu.SemaphoreType.DMA((ROUNDS, 2)),
-            pltpu.SemaphoreType.DMA((ROUNDS, 2)),
-            pltpu.SemaphoreType.DMA((12,)),
-            pltpu.SemaphoreType.DMA((12,)),
+            pltpu.SemaphoreType.DMA((ROUNDS, 3)),
+            pltpu.SemaphoreType.DMA((ROUNDS, 3)),
+            pltpu.SemaphoreType.DMA((4,)),
+            pltpu.SemaphoreType.DMA((4,)),
+            pltpu.SemaphoreType.DMA((16,)),
+            pltpu.SemaphoreType.DMA((16,)),
+            pltpu.SemaphoreType.DMA((15,)),
+            pltpu.SemaphoreType.DMA((15,)),
             pltpu.SemaphoreType.DMA((12,)),
         ],
         compiler_params=pltpu.CompilerParams(

time: 116 us -> 107 us (0.922)
  Pallas kernels: 109 us -> 99.7 us
    pallas_call x1, Pallas kernels: 109 us -> 99.7 us  [shards(): pl.pallas_call(kernel, out_shape=(jax.ShapeDtypeStruct((ROWS, D), F32), j...]
where the time goes in v3:
time: 107 us
  Pallas kernels  99.7 us (93%)
  local copies, waits for them, and re-layouts  5.68 us (5%)
    pallas_call x1, Pallas kernels, shards(): pl.pallas_call(kernel, out_shape=(jax.ShapeDtypeStruct((ROWS, D), F32), j...  99.7 us
    unnamed x7, local copies, waits for them, and re-layouts  5.68 us

profile of v3, /device:TPU:1, one launch (start us, length us, event | category | flops | bytes accessed | tf_op | source)
XLA Modules:
  0.0 106.7 jit_solution(8171491232028187487)
XLA Ops:
  0.6 99.7 %shard_map.129 = (f32[256,400]{1,0:T(8,128)}, f32[1,256]{1,0:T(1,128)}, f32[1300,400]{1,0:T(8,128)}, f32[1,1300]{1,0:T(1,128)}) custom-call(s32[2]{0:T(128)} %masks_hbm.1, s32[2,128]{1,0:T(2,128)} %src_hbm.1, s32[2,128]{1,0:T(2,128)} %rel_hbm.1, s32[2]{0:T(128)} %bitcast.9, f32[400,256]{1,0:T(8,128)} %bitcast.6, f32[1,256]{1,0:T(1,128)} %bitcast.7, ...), custom_call_target="tpu_custom_call" | custom-call | tf_op jit(solution)/shard_map/pallas_call | solution.py:550
  100.4 2.0 %copy.14 = f32[256,400]{0,1:T(8,128)} copy(f32[256,400]{1,0:T(8,128)} %get-tuple-element.12) | data formatting | bytes 819200
  102.3 0.0 copy-start
  102.3 0.0 copy-start.1
  102.3 3.1 %copy.15 = f32[1300,400]{0,1:T(8,128)} copy(f32[1300,400]{1,0:T(8,128)} %get-tuple-element.14) | data formatting | bytes 4160000
  105.5 0.0 copy-done
  105.5 0.6 reduce
  106.1 0.0 copy-done.1
  106.1 0.6 copy.17
Async XLA Ops:
  102.3 3.1 %copy-start = (f32[1,1300]{1,0:T(1,128)S(1)}, f32[1,1300]{1,0:T(1,128)}, u32[]{:S(2)}) copy-start(f32[1,1300]{1,0:T(1,128)} %get-tuple-element.11) | copy-start | bytes 15604
  102.3 3.8 %copy-start.1 = (f32[1,256]{1,0:T(1,128)S(1)}, f32[1,256]{1,0:T(1,128)}, u32[]{:S(2)}) copy-start(f32[1,256]{1,0:T(1,128)} %get-tuple-element.9) | copy-start | bytes 3076

commit v4 on v3

--- a/solution.py
+++ b/solution.py
@@ -15,6 +15,8 @@
 LEFT = D - 384
 CHIPS = 128
 TILES = 76
+ROW_TILES = 51
+VEC_TILES = 25
 REL_PAD = 1408
 BLOCK = 1304
 GROUP = 168
@@ -76,8 +78,12 @@
 )
 
 
-def carrier(tile):
-    return (5 * tile) // 3
+def row_carrier(tile):
+    return (5 * tile) // 2
+
+
+def vec_carrier(tile):
+    return 5 * (tile - ROW_TILES) + 1
 
 
 def kernel(
@@ -88,13 +94,11 @@
     emb_hbm,
     state_hbm,
     relations_hbm,
-    rel_state_hbm,
     dst_hbm,
     neg_hbm,
     emb_out,
     state_out,
-    rel_out,
-    rel_state_out,
+    gathered,
     masks,
     src_ids,
     rel_ids,
@@ -102,7 +106,6 @@
     emb_in,
     state_in,
     rel_in,
-    rel_state_in,
     src_rows,
     rel_rows,
     dst_rows,
@@ -118,20 +121,20 @@
     grads,
     is_rel,
     packed,
-    state_col,
     x1,
     held_0,
     held_1,
     x2,
-    arrived_0,
-    arrived_1,
+    rows_0,
+    rows_1,
+    vecs_0,
+    vecs_1,
     t0,
     r0,
     t1,
     ra,
     t3,
     rz,
-    gathered,
     send,
     recv,
     sum_send,
@@ -153,7 +156,6 @@
                 (masks_hbm, masks),
                 (counts_hbm, counts),
                 (state_hbm, state_in),
-                (rel_state_hbm, rel_state_in),
                 (src_hbm, src_rows),
                 (rel_hbm, rel_rows),
                 (dst_hbm, dst_rows),
@@ -169,20 +171,44 @@
     x = (me // 8) % 4
     z = me // 32
     chip = me // 2
-    mine = (3 * chip + 2) // 5
-    active = jnp.logical_and(carrier(mine) == chip, mine < TILES)
+    row_mine = (2 * chip + 1) // 5
+    vec_mine = ROW_TILES + chip // 5
+    has_row = jnp.logical_and(row_carrier(row_mine) == chip, row_mine < ROW_TILES)
+    has_vec = jnp.logical_and(vec_carrier(vec_mine) == chip, vec_mine < TILES)
+    active = jnp.logical_or(has_row, has_vec)
     idle = jnp.logical_not(active)
 
     def plane(step):
         return (z + 4 + ((step + 1) // 2) * (1 - 2 * (step % 2))) % 8
 
-    def first_tile(at):
-        return (48 * at + 4) // 5
-
-    def over_tiles(go):
+    def over_rows(go):
+        def first(at):
+            return (32 * at + 4) // 5
+
         def one_plane(step, _):
             at = plane(step)
-            lax.fori_loop(first_tile(at), jnp.minimum(first_tile(at + 1), TILES), go, 0)
+
+            def one(i, _):
+                go(i, row_carrier(i))
+                return 0
+
+            lax.fori_loop(first(at), jnp.minimum(first(at + 1), ROW_TILES), one, 0)
+            return 0
+
+        lax.fori_loop(0, 8, one_plane, 0)
+
+    def over_vecs(go):
+        def first(at):
+            return (16 * at + 3) // 5
+
+        def one_plane(step, _):
+            at = plane(step)
+
+            def one(i, _):
+                go(ROW_TILES + i, vec_carrier(ROW_TILES + i))
+                return 0
+
+            lax.fori_loop(first(at), jnp.minimum(first(at + 1), VEC_TILES), one, 0)
             return 0
 
         lax.fori_loop(0, 8, one_plane, 0)
@@ -216,9 +242,8 @@
         lax.fori_loop(0, 16, tell_chip, 0)
         return 0
 
-    def tell_carrier(i, _):
-        tell(2 * carrier(i) + c)
-        return 0
+    def tell_carrier(i, to):
+        tell(2 * to + c)
 
     @pl.when(active)
     def _():
@@ -226,7 +251,8 @@
 
     @pl.when(idle)
     def _():
-        over_tiles(tell_carrier)
+        over_rows(tell_carrier)
+        over_vecs(tell_carrier)
 
     for to in places[:-1]:
         tell(at_place(to))
@@ -276,10 +302,12 @@
         pack(r, 0, table[0:128, :])
         pack(r, 25, table[128:256, :])
 
-    def pack_vectors(r, rows):
+    def pack_vectors(r):
+        vec[...] = (srcs[r] * rels[r]).astype(BF16)
+        pack(r, ROW_TILES, vec[...])
+
+    def pack_meta(r, rows):
         dst, live, hits = rows
-        vec[...] = (srcs[r] * rels[r]).astype(BF16)
-        pack(r, 50, vec[...])
         high = jnp.floor(hits * (1.0 / 16.0))
         low = hits - 16.0 * high
         extras = (dst, live, high[:, :128], high[:, 128:], low[:, :128], low[:, 128:])
@@ -287,17 +315,12 @@
         meta = jnp.zeros((16, 128), F32)
         for n, extra in enumerate(extras):
             meta = jnp.where(sub == n, extra, meta)
-        x1[r, 75] = meta.astype(BF16)
-
-    def exchange(r, mask, during):
+        x1[r, 50] = meta.astype(BF16)
+
+    def send_out(r, over):
         held = (held_0, held_1)[r]
-        arrived = (arrived_0, arrived_1)[r]
-        chip_mask = lax.shift_right_logical(mask, 1)
-        side = lax.bitwise_and(mask, 1)
-
-        def outward(i, _):
-            to = carrier(i)
-
+
+        def outward(i, to):
             @pl.when(to != chip)
             def _():
                 remote(x1.at[r, i], held.at[chip], send.at[r, 0], recv.at[r, 0], 2 * to + c).start()
@@ -306,43 +329,40 @@
             def _():
                 held[chip] = x1[r, i]
 
+        over(outward)
+
+    def relay(r, mask, arrived, mine, sem):
+        held = (held_0, held_1)[r]
+        chip_mask = lax.shift_right_logical(mask, 1)
+        await_bytes(held.at[pl.ds(0, CHIPS - 1)], recv.at[r, 0])
+
+        def onward(step, _):
+            base = 16 * plane(step)
+            for n in range(16):
+                x2[r, base + n] = held[lax.bitwise_xor(chip_mask, base + n)]
+            for n in places:
+                to = base + n
+
+                @pl.when(to != chip)
+                def _():
+                    remote(x2.at[r, to], arrived.at[0, mine], send.at[r, 1], recv.at[r, sem], 2 * to + c).start()
+
             return 0
 
-        over_tiles(outward)
-        during()
-
-        @pl.when(active)
+        lax.fori_loop(0, 8, onward, 0)
+        arrived[0, mine] = x2[r, chip]
+
+    def take_in(r, has, arrived, count, sem):
+        @pl.when(has)
         def _():
-            await_bytes(held.at[pl.ds(0, CHIPS - 1)], recv.at[r, 0])
-
-            def onward(step, _):
-                base = 16 * plane(step)
-                for n in range(16):
-                    x2[r, base + n] = held[lax.bitwise_xor(chip_mask, base + n)]
-                for n in places:
-                    to = base + n
-
-                    @pl.when(to != chip)
-                    def _():
-                        remote(x2.at[r, to], arrived.at[0, mine], send.at[r, 1], recv.at[r, 1], 2 * to + c).start()
-
-                return 0
-
-            lax.fori_loop(0, 8, onward, 0)
-            arrived[0, mine] = x2[r, chip]
-            await_bytes(arrived.at[0, pl.ds(0, TILES - 1)], recv.at[r, 1])
-
-        @pl.when(idle)
+            await_bytes(arrived.at[0, pl.ds(0, count - 1)], recv.at[r, sem])
+
+        @pl.when(jnp.logical_not(has))
         def _():
-            await_bytes(arrived.at[0], recv.at[r, 1])
-
-        remote(arrived.at[0], arrived.at[1], send.at[r, 2], recv.at[r, 2], other).start()
-        await_bytes(arrived.at[1], recv.at[r, 2])
-
-        unpack(arrived, side, 0, far_table, 0)
-        unpack(arrived, side, 25, far_table, 128)
-        unpack(arrived, side, 50, far_vec, 0)
-        return arrived[side, 75].astype(F32)
+            await_bytes(arrived.at[0], recv.at[r, sem])
+
+        remote(arrived.at[0], arrived.at[1], send.at[r, sem + 1], recv.at[r, sem + 1], other).start()
+        await_bytes(arrived.at[1], recv.at[r, sem + 1])
 
     def sent(r):
         @pl.when(active)
@@ -354,7 +374,8 @@
         def _():
             await_bytes(x1.at[r], send.at[r, 0])
 
-        await_bytes(x1.at[r], send.at[r, 2])
+        await_bytes(x1.at[r, pl.ds(0, ROW_TILES)], send.at[r, 2])
+        await_bytes(x1.at[r, pl.ds(0, VEC_TILES)], send.at[r, 4])
 
     def coefficients(vectors, rows, ends):
         dst, live, hits = ends
@@ -377,6 +398,12 @@
                 128 * j : 128 * j + depth, 128 * i : 128 * i + 128
             ].T
     pack_table(0)
+    buckets = [bucket_rows(r) for r in range(ROUNDS)]
+    for r in range(ROUNDS):
+        pack_meta(r, buckets[r])
+    state = jnp.concatenate([as_column(state_in[:, :128]), as_column(state_in[:, 128:])], axis=0)
+
+    gather_srcs(0)
     relations[:, 384:] = jnp.zeros((REL_PAD, 128), F32)
     for j in range(4):
         depth = min(128, D - 128 * j)
@@ -386,11 +413,9 @@
             if width < 128:
                 part = jnp.concatenate([part, jnp.ones((depth, 128 - width), F32)], axis=1)
             relations[128 * i : 128 * i + 128, 128 * j : 128 * j + depth] = part.T
-    gather_rels(0)
-    gather_srcs(0)
-    near = bucket_rows(0)
-    pack_vectors(0, near)
-    state = jnp.concatenate([as_column(state_in[:, :128]), as_column(state_in[:, 128:])], axis=0)
+    for r in range(ROUNDS):
+        gather_rels(r)
+    pack_vectors(0)
 
     @pl.when(active)
     def _():
@@ -399,16 +424,6 @@
     @pl.when(idle)
     def _():
         pl.semaphore_wait(barrier, TILES + 23)
-
-    def prepare():
-        gather_rels(1)
-        later.append(bucket_rows(1))
-        for n in range(11):
-            width = min(128, NREL - 128 * n)
-            part = rel_state_in[128 * n : 128 * n + width].reshape(1, width)
-            if width < 128:
-                part = jnp.concatenate([part, jnp.ones((1, 128 - width), F32)], axis=1)
-            state_col[128 * n : 128 * n + 128, :] = as_column(part)
 
     def prepare_sum():
         ids = jnp.concatenate([rel_rows[0:1, :], rel_rows[1:2, :]], axis=1)
@@ -416,14 +431,38 @@
             at = GROUP * g
             is_rel[at : at + GROUP, :] = (iota((GROUP, ROUNDS * EDGES), 0) + at == ids).astype(BF16)
 
-    later = []
     for r in range(ROUNDS):
-        meta = exchange(r, masks[r], prepare if r == 0 else prepare_sum)
+        mask = masks[r]
+        side = lax.bitwise_and(mask, 1)
+        far_rows = (rows_0, rows_1)[r]
+        far_vecs = (vecs_0, vecs_1)[r]
+        send_out(r, over_rows)
+        if r > 0:
+            gather_srcs(r)
+            pack_vectors(r)
+        send_out(r, over_vecs)
+        if r == 0:
+            prepare_sum()
+
+        @pl.when(has_row)
+        def _():
+            relay(r, mask, far_rows, row_mine, 1)
+
+        @pl.when(has_vec)
+        def _():
+            relay(r, mask, far_vecs, vec_mine - ROW_TILES, 3)
+
+        take_in(r, has_row, far_rows, ROW_TILES, 1)
+        unpack(far_rows, side, 0, far_table, 0)
+        unpack(far_rows, side, 25, far_table, 128)
+        meta = far_rows[side, 50].astype(F32)
         hits = jnp.concatenate([16.0 * meta[n : n + 1] + meta[n + 2 : n + 3] for n in (2, 3)], axis=1)
         far = (meta[0:1], meta[1:2], hits)
 
-        high, low = coefficients(vec[...], far_table[...], near)
+        high, low = coefficients(vec[...], far_table[...], buckets[r])
         pulled = (dot(high, far_table[...]) + dot(low, far_table[...])).astype(BF16).astype(F32)
+        take_in(r, has_vec, far_vecs, VEC_TILES, 3)
+        unpack(far_vecs, side, 0, far_vec, 0)
         high, low = coefficients(far_vec[...], table[...], far)
         pushed = (dot(high, far_vec[...], 0, 0) + dot(low, far_vec[...], 0, 0)).astype(BF16).astype(F32)
 
@@ -435,9 +474,6 @@
         emb[...] = emb[...] - learning_rate * grad / jnp.sqrt(state)
         if r + 1 < ROUNDS:
             pack_table(r + 1)
-            gather_srcs(r + 1)
-            near = later[r]
-            pack_vectors(r + 1, near)
 
     tail = jnp.zeros((GROUP, 128), F32)
     for g in range(8):
@@ -495,30 +531,13 @@
         if k < 15:
             await_bytes(piece, gather_recv.at[k])
         remote(piece, piece, sum_send.at[3], sum_recv.at[3], other).start()
-    emb_out[...] = emb[:, :D]
+    for j in range(4):
+        depth = min(128, D - 128 * j)
+        for i in range(2):
+            part = emb[128 * i : 128 * i + 128, 128 * j : 128 * j + 128].T
+            emb_out[128 * j : 128 * j + depth, 128 * i : 128 * i + 128] = part[:depth]
     state_out[...] = jnp.concatenate([as_row(state[:128]), as_row(state[128:])], axis=1)
     await_bytes(gathered.at[pl.ds(0, 128)], sum_recv.at[3])
-
-    packed[...] = gathered[...].astype(F32).reshape(PACKED, 128)
-    for g in range(8):
-        rows = min(GROUP, NREL - GROUP * g)
-        at = GROUP * g
-        parts = [packed[BLOCK * n + at : BLOCK * n + at + rows, :] for n in range(3)]
-        end = packed[3 * BLOCK : 3 * BLOCK + GROUP, :]
-        end = (pltpu.roll(end, 128 - LEFT * g, 1) if g else end)[:rows, :LEFT]
-        squares = parts[0] * parts[0] + parts[1] * parts[1] + parts[2] * parts[2]
-        mean = jnp.sum(squares, axis=1, keepdims=True) + jnp.sum(end * end, axis=1, keepdims=True)
-        fresh = state_col[at : at + rows, :] + mean * (1.0 / D)
-        state_col[at : at + rows, :] = fresh
-        root = jnp.sqrt(fresh)
-        for n in range(3):
-            cols = slice(128 * n, 128 * n + 128)
-            rel_out[at : at + rows, cols] = relations[at : at + rows, cols] - learning_rate * parts[n] / root
-        rel_out[at : at + rows, 384:] = relations[at : at + rows, 384:D] - learning_rate * end / root
-    for n in range(11):
-        width = min(128, NREL - 128 * n)
-        row = as_row(state_col[128 * n : 128 * n + 128, :])
-        rel_state_out[:, 128 * n : 128 * n + width] = row[:, :width]
 
     for r in range(ROUNDS):
         sent(r)
@@ -528,6 +547,80 @@
         await_bytes(gathered.at[pl.ds(0, tiles)], sum_send.at[n])
     for k in range(15):
         await_bytes(gathered.at[pl.ds(0, 8)], gather_send.at[k])
+
+
+def finish(
+    emb_hbm,
+    state_hbm,
+    sums_hbm,
+    rel_hbm,
+    rel_state_hbm,
+    emb_out,
+    state_out,
+    rel_out,
+    rel_state_out,
+    sums,
+    rel_in,
+    state_in,
+    rel_state_in,
+    packed,
+    tails,
+    rel_new,
+    state_new,
+    rel_state_new,
+    emb_kept,
+    sems,
+):
+    loads = [
+        pltpu.make_async_copy(sums_hbm, sums, sems.at[0]),
+        pltpu.make_async_copy(rel_state_hbm, rel_state_in, sems.at[1]),
+        pltpu.make_async_copy(rel_hbm, rel_in, sems.at[2]),
+        pltpu.make_async_copy(state_hbm, state_in, sems.at[3]),
+    ]
+    loads.append(pltpu.make_async_copy(emb_hbm, emb_kept, sems.at[4]))
+    for load in loads:
+        load.start()
+    for load in loads:
+        load.wait()
+    state_new[...] = state_in[...].reshape(ROWS)
+    stores = [
+        pltpu.make_async_copy(state_new, state_out, sems.at[5]),
+        pltpu.make_async_copy(emb_kept, emb_out, sems.at[8]),
+    ]
+    for store in stores:
+        store.start()
+    packed[...] = sums[...].astype(F32).reshape(PACKED, 128)
+    end = packed[3 * BLOCK : 3 * BLOCK + GROUP, :]
+    inside = iota((GROUP, 128), 1) < LEFT
+    for g in range(8):
+        part = pltpu.roll(end, 128 - LEFT * g, 1) if g else end
+        tails[GROUP * g : GROUP * g + GROUP, :] = jnp.where(inside, part, 0.0)
+    tails[8 * GROUP :, :] = jnp.zeros((REL_PAD - 8 * GROUP, 128), F32)
+    for i in range(11):
+        at = 128 * i
+        width = min(128, NREL - at)
+        rows = min(128, BLOCK - at)
+        parts = [packed[BLOCK * n + at : BLOCK * n + at + rows, :] for n in range(3)] + [tails[at : at + rows, :]]
+        if rows < 128:
+            parts = [jnp.concatenate([part, jnp.zeros((128 - rows, 128), F32)], axis=0) for part in parts]
+        old = rel_state_in[at : at + width].reshape(1, width)
+        if width < 128:
+            old = jnp.concatenate([old, jnp.ones((1, 128 - width), F32)], axis=1)
+        squares = parts[0] * parts[0] + parts[1] * parts[1] + parts[2] * parts[2] + parts[3] * parts[3]
+        fresh = old + as_row(jnp.sum(squares, axis=1, keepdims=True)) * (1.0 / D)
+        rel_state_new[at : at + width] = fresh[:, :width].reshape(width)
+        root = jnp.sqrt(fresh)
+        for n in range(4):
+            depth = min(128, D - 128 * n)
+            change = learning_rate * parts[n].T[:depth] / root
+            cols = slice(128 * n, 128 * n + depth)
+            rel_new[cols, at : at + width] = rel_in[cols, at : at + width] - change[:, :width]
+    stores.append(pltpu.make_async_copy(rel_new, rel_out, sems.at[6]))
+    stores.append(pltpu.make_async_copy(rel_state_new, rel_state_out, sems.at[7]))
+    for store in stores[2:]:
+        store.start()
+    for store in stores:
+        store.wait()
 
 
 def shards(
@@ -547,16 +640,16 @@
     def tiles(*lead):
         return pltpu.VMEM(lead + (16, 128), BF16)
 
-    new_rows, new_state, new_relations, new_relation_state = pl.pallas_call(
+    hbm = pl.BlockSpec(memory_space=pltpu.HBM)
+    rows_t, state, sums = pl.pallas_call(
         kernel,
         out_shape=(
-            jax.ShapeDtypeStruct((ROWS, D), F32),
+            jax.ShapeDtypeStruct((D, ROWS), F32),
             jax.ShapeDtypeStruct((1, ROWS), F32),
-            jax.ShapeDtypeStruct((NREL, D), F32),
-            jax.ShapeDtypeStruct((1, NREL), F32),
+            jax.ShapeDtypeStruct((256, 16, 128), BF16),
         ),
-        in_specs=[pl.BlockSpec(memory_space=pltpu.HBM)] * 10,
-        out_specs=(vmem,) * 4,
+        in_specs=[hbm] * 9,
+        out_specs=(vmem,) * 3,
         scratch_shapes=[
             pltpu.SMEM((ROUNDS,), jnp.int32),
             pltpu.SMEM((ROUNDS, EDGES), jnp.int32),
@@ -565,7 +658,6 @@
             pltpu.VMEM((D, ROWS), F32),
             pltpu.VMEM((1, ROWS), F32),
             pltpu.VMEM((D, NREL), F32),
-            pltpu.VMEM((NREL,), F32),
             pltpu.VMEM((ROUNDS, EDGES), jnp.int32),
             pltpu.VMEM((ROUNDS, EDGES), jnp.int32),
             pltpu.VMEM((ROUNDS, EDGES), jnp.int32),
@@ -581,22 +673,22 @@
             pltpu.VMEM((ROUNDS * EDGES, WIDE), BF16),
             pltpu.VMEM((8 * GROUP, ROUNDS * EDGES), BF16),
             pltpu.VMEM((PACKED, 128), F32),
-            pltpu.VMEM((REL_PAD, 1), F32),
             tiles(ROUNDS, TILES),
             tiles(CHIPS),
             tiles(CHIPS),
             tiles(ROUNDS, CHIPS),
-            tiles(2, TILES),
-            tiles(2, TILES),
+            tiles(2, ROW_TILES),
+            tiles(2, ROW_TILES),
+            tiles(2, VEC_TILES),
+            tiles(2, VEC_TILES),
             tiles(256),
             tiles(128),
             tiles(128),
             tiles(16, 8),
             tiles(8),
             tiles(8),
-            tiles(256),
-            pltpu.SemaphoreType.DMA((ROUNDS, 3)),
-            pltpu.SemaphoreType.DMA((ROUNDS, 3)),
+            pltpu.SemaphoreType.DMA((ROUNDS, 5)),
+            pltpu.SemaphoreType.DMA((ROUNDS, 5)),
             pltpu.SemaphoreType.DMA((4,)),
             pltpu.SemaphoreType.DMA((4,)),
             pltpu.SemaphoreType.DMA((16,)),
@@ -616,11 +708,35 @@
         embeddings.T,
         entity_state.reshape(1, ROWS),
         relations.T,
-        relation_state,
         edge_dst,
         neg_rows,
     )
-    return (new_rows, new_state.reshape(ROWS), new_relations, new_relation_state.reshape(NREL))
+    new_rows, new_state, new_relations, new_relation_state = pl.pallas_call(
+        finish,
+        out_shape=(
+            jax.ShapeDtypeStruct((D, ROWS), F32),
+            jax.ShapeDtypeStruct((ROWS,), F32),
+            jax.ShapeDtypeStruct((D, NREL), F32),
+            jax.ShapeDtypeStruct((NREL,), F32),
+        ),
+        in_specs=[hbm] * 5,
+        out_specs=(hbm,) * 4,
+        scratch_shapes=[
+            tiles(256),
+            pltpu.VMEM((D, NREL), F32),
+            pltpu.VMEM((1, ROWS), F32),
+            pltpu.VMEM((NREL,), F32),
+            pltpu.VMEM((PACKED, 128), F32),
+            pltpu.VMEM((REL_PAD, 128), F32),
+            pltpu.VMEM((D, NREL), F32),
+            pltpu.VMEM((ROWS,), F32),
+            pltpu.VMEM((NREL,), F32),
+            pltpu.VMEM((D, ROWS), F32),
+            pltpu.SemaphoreType.DMA((9,)),
+        ],
+        compiler_params=pltpu.CompilerParams(vmem_limit_bytes=60 * 1024 * 1024),
+    )(rows_t, state, sums, relations.T, relation_state)
+    return (new_rows.T, new_state, new_relations.T, new_relation_state)
 
 
 def solution(mesh):

time: 107 us -> 102 us (0.953)
  local copies, waits for them, and re-layouts: 5.68 us -> 0 us
  Pallas kernels: 99.7 us -> 102 us
    unnamed x7 -> x0, local copies, waits for them, and re-layouts: 5.68 us -> none
    pallas_call x1 -> x2, Pallas kernels: 99.7 us -> 102 us  [the longest x1 97.3 us: shards(): pl.pallas_call(kernel, out_shape=(jax.ShapeDtypeStruct((D, ROWS), F32), j...]
where the time goes in v4:
time: 102 us
  Pallas kernels  102 us (100%)
    pallas_call x1, Pallas kernels, shards(): pl.pallas_call(kernel, out_shape=(jax.ShapeDtypeStruct((D, ROWS), F32), j...  97.3 us
    pallas_call x1, Pallas kernels, shards(): pl.pallas_call(finish, out_shape=(jax.ShapeDtypeStruct((D, ROWS), F32), j...  4.35 us

profile of v4, /device:TPU:1, one launch (start us, length us, event | category | flops | bytes accessed | tf_op | source)
XLA Modules:
  0.0 102.2 jit_solution(11164583602565028088)
XLA Ops:
  0.6 97.3 %shard_map.129 = (f32[400,256]{1,0:T(8,128)}, f32[1,256]{1,0:T(1,128)}, bf16[256,16,128]{2,1,0:T(8,128)(2,1)}) custom-call(s32[2]{0:T(128)} %masks_hbm.1, s32[2,128]{1,0:T(2,128)} %src_hbm.1, s32[2,128]{1,0:T(2,128)} %rel_hbm.1, s32[2]{0:T(128)} %bitcast.10, f32[400,256]{1,0:T(8,128)} %bitcast.8, f32[1,256]{1,0:T(1,128)} %bitcast.9, f32[400,1300]{1,0:T(8,128)} %bitcast.6, ...), custom_call_target="tpu_custom_call" | custom-call | tf_op jit(solution)/shard_map/pallas_call | solution.py:644
  97.9 4.4 %shard_map.130 = (f32[400,256]{1,0:T(8,128)}, f32[256]{0:T(256)}, f32[400,1300]{1,0:T(8,128)}, f32[1300]{0:T(1024)}) custom-call(f32[400,256]{1,0:T(8,128)} %get-tuple-element.11.emb_hbm, f32[1,256]{1,0:T(1,128)} %get-tuple-element.12.state_hbm, bf16[256,16,128]{2,1,0:T(8,128)(2,1)} %get-tuple-element.13.sums_hbm, f32[400,1300]{1,0:T(8,128)} %bitcast.7, ...), custom_call_target="tpu_custom_call" | custom-call | tf_op jit(solution)/shard_map/pallas_call | solution.py:714

commit v5 on v4

--- a/solution.py
+++ b/solution.py
@@ -163,8 +163,6 @@
             )
         )
     ]
-    for load in loads:
-        load.start()
     me = lax.axis_index("dom")
     c = me % 2
     y = (me // 2) % 4
@@ -259,6 +257,8 @@
     for step in range(7):
         tell(at_z(plane(step)))
     tell(other)
+    for load in loads:
+        load.start()
 
     def gather_rels(r):
         for e in range(EDGES):
@@ -362,7 +362,6 @@
             await_bytes(arrived.at[0], recv.at[r, sem])
 
         remote(arrived.at[0], arrived.at[1], send.at[r, sem + 1], recv.at[r, sem + 1], other).start()
-        await_bytes(arrived.at[1], recv.at[r, sem + 1])
 
     def sent(r):
         @pl.when(active)
@@ -440,19 +439,24 @@
         if r > 0:
             gather_srcs(r)
             pack_vectors(r)
-        send_out(r, over_vecs)
-        if r == 0:
+        if r + 1 < ROUNDS:
+            send_out(r, over_vecs)
             prepare_sum()
 
         @pl.when(has_row)
         def _():
             relay(r, mask, far_rows, row_mine, 1)
 
-        @pl.when(has_vec)
-        def _():
-            relay(r, mask, far_vecs, vec_mine - ROW_TILES, 3)
+        if r + 1 == ROUNDS:
+            send_out(r, over_vecs)
+        else:
+
+            @pl.when(has_vec)
+            def _():
+                relay(r, mask, far_vecs, vec_mine - ROW_TILES, 3)
 
         take_in(r, has_row, far_rows, ROW_TILES, 1)
+        await_bytes(far_rows.at[1], recv.at[r, 2])
         unpack(far_rows, side, 0, far_table, 0)
         unpack(far_rows, side, 25, far_table, 128)
         meta = far_rows[side, 50].astype(F32)
@@ -460,19 +464,28 @@
         far = (meta[0:1], meta[1:2], hits)
 
         high, low = coefficients(vec[...], far_table[...], buckets[r])
+        if r + 1 < ROUNDS:
+            take_in(r, has_vec, far_vecs, VEC_TILES, 3)
         pulled = (dot(high, far_table[...]) + dot(low, far_table[...])).astype(BF16).astype(F32)
-        take_in(r, has_vec, far_vecs, VEC_TILES, 3)
-        unpack(far_vecs, side, 0, far_vec, 0)
-        high, low = coefficients(far_vec[...], table[...], far)
-        pushed = (dot(high, far_vec[...], 0, 0) + dot(low, far_vec[...], 0, 0)).astype(BF16).astype(F32)
-
         grads[r * EDGES : (r + 1) * EDGES, :] = (pulled * srcs[r]).astype(BF16)
-        is_src = (iota((ROWS, EDGES), 0) == src_rows[r : r + 1, :]).astype(BF16)
-        high, low = halves(pulled * rels[r])
-        grad = pushed + dot(is_src, high) + dot(is_src, low)
-        state = state + jnp.sum(grad * grad, axis=1, keepdims=True) * (1.0 / D)
-        emb[...] = emb[...] - learning_rate * grad / jnp.sqrt(state)
+
+        def update_rows(r, state, pulled, far, far_vecs, side):
+            is_src = (iota((ROWS, EDGES), 0) == src_rows[r : r + 1, :]).astype(BF16)
+            high, low = halves(pulled * rels[r])
+            grad = dot(is_src, high) + dot(is_src, low)
+            if r + 1 == ROUNDS:
+                take_in(r, has_vec, far_vecs, VEC_TILES, 3)
+            await_bytes(far_vecs.at[1], recv.at[r, 4])
+            unpack(far_vecs, side, 0, far_vec, 0)
+            high, low = coefficients(far_vec[...], table[...], far)
+            pushed = dot(high, far_vec[...], 0, 0) + dot(low, far_vec[...], 0, 0)
+            grad = grad + pushed.astype(BF16).astype(F32)
+            state = state + jnp.sum(grad * grad, axis=1, keepdims=True) * (1.0 / D)
+            emb[...] = emb[...] - grad * (learning_rate / jnp.sqrt(state))
+            return state
+
         if r + 1 < ROUNDS:
+            state = update_rows(r, state, pulled, far, far_vecs, side)
             pack_table(r + 1)
 
     tail = jnp.zeros((GROUP, 128), F32)
@@ -486,18 +499,27 @@
         tail = tail + (pltpu.roll(end, LEFT * g, 1) if g else end)
     packed[3 * BLOCK : 3 * BLOCK + GROUP, :] = tail
     packed[3 * BLOCK + GROUP :, :] = jnp.zeros((PACKED - 3 * BLOCK - GROUP, 128), F32)
-    t0[...] = packed[...].reshape(256, 16, 128).astype(BF16)
+
+    def partial(half, to):
+        rows = pl.ds(pl.multiple_of(2048 * half + 128 * to, 128), 128)
+        return packed[rows, :].reshape(8, 16, 128)
 
     for k, to in enumerate(places):
-        piece = pl.ds((1 - c) * 128 + 8 * to, 8)
-        remote(t0.at[piece], r0.at[pl.ds(8 * to, 8)], core_send.at[k], core_recv.at[k], other).start()
+        piece = pl.ds(8 * to, 8)
+        t0[piece] = partial(1 - c, to).astype(BF16)
+        remote(t0.at[piece], r0.at[piece], core_send.at[k], core_recv.at[k], other).start()
     for k, to in enumerate(places):
         piece = pl.ds(8 * to, 8)
         await_bytes(r0.at[piece], core_recv.at[k])
-        t1[piece] = (t0[pl.ds(c * 128 + 8 * to, 8)].astype(F32) + r0[piece].astype(F32)).astype(BF16)
+        t1[piece] = (partial(c, to) + r0[piece].astype(F32)).astype(BF16)
         if k < 15:
             remote(t1.at[piece], ra.at[place], sum_send.at[0], sum_recv.at[0], at_place(to)).start()
     ra[place] = t1[pl.ds(8 * place, 8)]
+
+    @pl.when(has_vec)
+    def _():
+        relay(r, mask, far_vecs, vec_mine - ROW_TILES, 3)
+
     await_bytes(ra.at[pl.ds(0, 15)], sum_recv.at[0])
 
     def added(ref, count):
@@ -526,6 +548,7 @@
         dx, dy = OFFSETS[k]
         back = OFFSETS.index((-dx % 4, -dy % 4))
         remote(own, own, gather_send.at[k], gather_recv.at[back], at_place(to)).start()
+    state = update_rows(r, state, pulled, far, far_vecs, side)
     for k, to in [(15, place)] + list(enumerate(places[:-1])):
         piece = gathered.at[pl.ds(c * 128 + 8 * to, 8)]
         if k < 15:
@@ -609,10 +632,10 @@
         squares = parts[0] * parts[0] + parts[1] * parts[1] + parts[2] * parts[2] + parts[3] * parts[3]
         fresh = old + as_row(jnp.sum(squares, axis=1, keepdims=True)) * (1.0 / D)
         rel_state_new[at : at + width] = fresh[:, :width].reshape(width)
-        root = jnp.sqrt(fresh)
+        scale = learning_rate / jnp.sqrt(fresh)
         for n in range(4):
             depth = min(128, D - 128 * n)
-            change = learning_rate * parts[n].T[:depth] / root
+            change = parts[n].T[:depth] * scale
             cols = slice(128 * n, 128 * n + depth)
             rel_new[cols, at : at + width] = rel_in[cols, at : at + width] - change[:, :width]
     stores.append(pltpu.make_async_copy(rel_new, rel_out, sems.at[6]))
@@ -681,7 +704,7 @@
             tiles(2, ROW_TILES),
             tiles(2, VEC_TILES),
             tiles(2, VEC_TILES),
-            tiles(256),
+            tiles(128),
             tiles(128),
             tiles(128),
             tiles(16, 8),

time: 102 us -> 101 us (level)
  Pallas kernels: 102 us -> 100 us
    pallas_call x1, Pallas kernels: 97.3 us -> 95.8 us  [shards(): pl.pallas_call(kernel, out_shape=(jax.ShapeDtypeStruct((D, ROWS), F32), j...]
where the time goes in v5:
time: 101 us
  Pallas kernels  100 us (99%)
    pallas_call x1, Pallas kernels, shards(): pl.pallas_call(kernel, out_shape=(jax.ShapeDtypeStruct((D, ROWS), F32), j...  95.8 us
    pallas_call x1, Pallas kernels, shards(): pl.pallas_call(finish, out_shape=(jax.ShapeDtypeStruct((D, ROWS), F32), j...  4.3 us

profile of v5, /device:TPU:1, one launch (start us, length us, event | category | flops | bytes accessed | tf_op | source)
XLA Modules:
  0.0 100.7 jit_solution(13040958298794671126)
XLA Ops:
  0.6 95.8 %shard_map.129 = (f32[400,256]{1,0:T(8,128)}, f32[1,256]{1,0:T(1,128)}, bf16[256,16,128]{2,1,0:T(8,128)(2,1)}) custom-call(s32[2]{0:T(128)} %masks_hbm.1, s32[2,128]{1,0:T(2,128)} %src_hbm.1, s32[2,128]{1,0:T(2,128)} %rel_hbm.1, s32[2]{0:T(128)} %bitcast.10, f32[400,256]{1,0:T(8,128)} %bitcast.8, f32[1,256]{1,0:T(1,128)} %bitcast.9, f32[400,1300]{1,0:T(8,128)} %bitcast.6, ...), custom_call_target="tpu_custom_call" | custom-call | tf_op jit(solution)/shard_map/pallas_call | solution.py:667
  96.4 4.3 %shard_map.130 = (f32[400,256]{1,0:T(8,128)}, f32[256]{0:T(256)}, f32[400,1300]{1,0:T(8,128)}, f32[1300]{0:T(1024)}) custom-call(f32[400,256]{1,0:T(8,128)} %get-tuple-element.11.emb_hbm, f32[1,256]{1,0:T(1,128)} %get-tuple-element.12.state_hbm, bf16[256,16,128]{2,1,0:T(8,128)(2,1)} %get-tuple-element.13.sums_hbm, f32[400,1300]{1,0:T(8,128)} %bitcast.7, ...), custom_call_target="tpu_custom_call" | custom-call | tf_op jit(solution)/shard_map/pallas_call | solution.py:737

commit v6 on v5

--- a/solution.py
+++ b/solution.py
@@ -530,19 +530,12 @@
 
     t3[...] = added(ra, 16)
     for step in range(7):
-        to = plane(step)
-        remote(t3.at[to], rz.at[z], sum_send.at[1], sum_recv.at[1], at_z(to)).start()
-    rz[z] = t3[z]
+        remote(t3, rz.at[z], sum_send.at[1], sum_recv.at[1], at_z(plane(step))).start()
+    rz[z] = t3[...]
     await_bytes(rz.at[pl.ds(0, 7)], sum_recv.at[1])
 
     base = c * 128 + 8 * place
-    spot = base + z
-    gathered[spot] = added(rz, 8)
-    for step in range(7):
-        to = plane(step)
-        remote(gathered.at[spot], gathered.at[spot], sum_send.at[2], sum_recv.at[2], at_z(to)).start()
-    await_bytes(gathered.at[pl.ds(0, 7)], sum_recv.at[2])
-
+    gathered[pl.ds(base, 8)] = added(rz, 8)
     own = gathered.at[pl.ds(base, 8)]
     for k, to in enumerate(places[:-1]):
         dx, dy = OFFSETS[k]
@@ -566,7 +559,7 @@
         sent(r)
     for k in range(16):
         await_bytes(r0.at[pl.ds(0, 8)], core_send.at[k])
-    for n, tiles in ((0, 120), (1, 7), (2, 7), (3, 128)):
+    for n, tiles in ((0, 120), (1, 56), (3, 128)):
         await_bytes(gathered.at[pl.ds(0, tiles)], sum_send.at[n])
     for k in range(15):
         await_bytes(gathered.at[pl.ds(0, 8)], gather_send.at[k])
@@ -603,7 +596,10 @@
     loads.append(pltpu.make_async_copy(emb_hbm, emb_kept, sems.at[4]))
     for load in loads:
         load.start()
-    for load in loads:
+    for load in loads[:2]:
+        load.wait()
+    packed[...] = sums[...].astype(F32).reshape(PACKED, 128)
+    for load in loads[2:]:
         load.wait()
     state_new[...] = state_in[...].reshape(ROWS)
     stores = [
@@ -612,7 +608,6 @@
     ]
     for store in stores:
         store.start()
-    packed[...] = sums[...].astype(F32).reshape(PACKED, 128)
     end = packed[3 * BLOCK : 3 * BLOCK + GROUP, :]
     inside = iota((GROUP, 128), 1) < LEFT
     for g in range(8):
@@ -709,7 +704,7 @@
             tiles(128),
             tiles(16, 8),
             tiles(8),
-            tiles(8),
+            tiles(8, 8),
             pltpu.SemaphoreType.DMA((ROUNDS, 5)),
             pltpu.SemaphoreType.DMA((ROUNDS, 5)),
             pltpu.SemaphoreType.DMA((4,)),

time: 101 us -> 98.7 us (0.977)
  Pallas kernels: 100 us -> 97.9 us
    pallas_call x1, Pallas kernels: 95.8 us -> 93.7 us  [shards(): pl.pallas_call(kernel, out_shape=(jax.ShapeDtypeStruct((D, ROWS), F32), j...]
where the time goes in v6:
time: 98.7 us; the launch traced here: 98.6 us
  Pallas kernels  97.9 us (99%)
    pallas_call x1, Pallas kernels, shards(): pl.pallas_call(kernel, out_shape=(jax.ShapeDtypeStruct((D, ROWS), F32), j...  93.7 us
    pallas_call x1, Pallas kernels, shards(): pl.pallas_call(finish, out_shape=(jax.ShapeDtypeStruct((D, ROWS), F32), j...  4.29 us

profile of v6, /device:TPU:1, one launch (start us, length us, event | category | flops | bytes accessed | tf_op | source)
XLA Modules:
  0.0 98.6 jit_solution(6423116474247564852)
XLA Ops:
  0.6 93.7 %shard_map.129 = (f32[400,256]{1,0:T(8,128)}, f32[1,256]{1,0:T(1,128)}, bf16[256,16,128]{2,1,0:T(8,128)(2,1)}) custom-call(s32[2]{0:T(128)} %masks_hbm.1, s32[2,128]{1,0:T(2,128)} %src_hbm.1, s32[2,128]{1,0:T(2,128)} %rel_hbm.1, s32[2]{0:T(128)} %bitcast.10, f32[400,256]{1,0:T(8,128)} %bitcast.8, f32[1,256]{1,0:T(1,128)} %bitcast.9, f32[400,1300]{1,0:T(8,128)} %bitcast.6, ...), custom_call_target="tpu_custom_call" | custom-call | tf_op jit(solution)/shard_map/pallas_call | solution.py:662
  94.3 4.3 %shard_map.130 = (f32[400,256]{1,0:T(8,128)}, f32[256]{0:T(256)}, f32[400,1300]{1,0:T(8,128)}, f32[1300]{0:T(1024)}) custom-call(f32[400,256]{1,0:T(8,128)} %get-tuple-element.11.emb_hbm, f32[1,256]{1,0:T(1,128)} %get-tuple-element.12.state_hbm, bf16[256,16,128]{2,1,0:T(8,128)(2,1)} %get-tuple-element.13.sums_hbm, f32[400,1300]{1,0:T(8,128)} %bitcast.7, ...), custom_call_target="tpu_custom_call" | custom-call | tf_op jit(solution)/shard_map/pallas_call | solution.py:732

commit v7 on v6

--- a/solution.py
+++ b/solution.py
@@ -541,11 +541,11 @@
         dx, dy = OFFSETS[k]
         back = OFFSETS.index((-dx % 4, -dy % 4))
         remote(own, own, gather_send.at[k], gather_recv.at[back], at_place(to)).start()
+    remote(own, own, sum_send.at[3], sum_recv.at[3], other).start()
     state = update_rows(r, state, pulled, far, far_vecs, side)
-    for k, to in [(15, place)] + list(enumerate(places[:-1])):
+    for k, to in enumerate(places[:-1]):
         piece = gathered.at[pl.ds(c * 128 + 8 * to, 8)]
-        if k < 15:
-            await_bytes(piece, gather_recv.at[k])
+        await_bytes(piece, gather_recv.at[k])
         remote(piece, piece, sum_send.at[3], sum_recv.at[3], other).start()
     for j in range(4):
         depth = min(128, D - 128 * j)
@@ -633,10 +633,13 @@
             change = parts[n].T[:depth] * scale
             cols = slice(128 * n, 128 * n + depth)
             rel_new[cols, at : at + width] = rel_in[cols, at : at + width] - change[:, :width]
-    stores.append(pltpu.make_async_copy(rel_new, rel_out, sems.at[6]))
+        if i in (3, 7, 10):
+            done = pl.ds(512 * (i // 4), min(512, NREL - 512 * (i // 4)))
+            part = pltpu.make_async_copy(rel_new.at[:, done], rel_out.at[:, done], sems.at[9 + i // 4])
+            part.start()
+            stores.append(part)
     stores.append(pltpu.make_async_copy(rel_state_new, rel_state_out, sems.at[7]))
-    for store in stores[2:]:
-        store.start()
+    stores[-1].start()
     for store in stores:
         store.wait()
 
@@ -750,7 +753,7 @@
             pltpu.VMEM((ROWS,), F32),
             pltpu.VMEM((NREL,), F32),
             pltpu.VMEM((D, ROWS), F32),
-            pltpu.SemaphoreType.DMA((9,)),
+            pltpu.SemaphoreType.DMA((12,)),
         ],
         compiler_params=pltpu.CompilerParams(vmem_limit_bytes=60 * 1024 * 1024),
     )(rows_t, state, sums, relations.T, relation_state)

time: 98.7 us -> 98.5 us (level)
  no operation moved by 1% of the time
where the time goes in v7:
time: 98.5 us
  Pallas kernels  97.8 us (99%)
    pallas_call x1, Pallas kernels, shards(): pl.pallas_call(kernel, out_shape=(jax.ShapeDtypeStruct((D, ROWS), F32), j...  93.7 us
    pallas_call x1, Pallas kernels, shards(): pl.pallas_call(finish, out_shape=(jax.ShapeDtypeStruct((D, ROWS), F32), j...  4.08 us

profile of v7, /device:TPU:1, one launch (start us, length us, event | category | flops | bytes accessed | tf_op | source)
XLA Modules:
  0.0 98.5 jit_solution(15088245817997215834)
XLA Ops:
  0.6 93.7 %shard_map.129 = (f32[400,256]{1,0:T(8,128)}, f32[1,256]{1,0:T(1,128)}, bf16[256,16,128]{2,1,0:T(8,128)(2,1)}) custom-call(s32[2]{0:T(128)} %masks_hbm.1, s32[2,128]{1,0:T(2,128)} %src_hbm.1, s32[2,128]{1,0:T(2,128)} %rel_hbm.1, s32[2]{0:T(128)} %bitcast.10, f32[400,256]{1,0:T(8,128)} %bitcast.8, f32[1,256]{1,0:T(1,128)} %bitcast.9, f32[400,1300]{1,0:T(8,128)} %bitcast.6, ...), custom_call_target="tpu_custom_call" | custom-call | tf_op jit(solution)/shard_map/pallas_call | solution.py:665
  94.4 4.1 %shard_map.130 = (f32[400,256]{1,0:T(8,128)}, f32[256]{0:T(256)}, f32[400,1300]{1,0:T(8,128)}, f32[1300]{0:T(1024)}) custom-call(f32[400,256]{1,0:T(8,128)} %get-tuple-element.11.emb_hbm, f32[1,256]{1,0:T(1,128)} %get-tuple-element.12.state_hbm, bf16[256,16,128]{2,1,0:T(8,128)(2,1)} %get-tuple-element.13.sums_hbm, f32[400,1300]{1,0:T(8,128)} %bitcast.7, ...), custom_call_target="tpu_custom_call" | custom-call | tf_op jit(solution)/shard_map/pallas_call | solution.py:735
